TPU v7x, 128 devices: a whole 4x4x4 slice. The times are simulated.
128 devices in a mesh: patch: 16 (over z_lo, x, core), head: 8 (over z_hi, y).
Axes of the slice: x: 4, y: 4, z: 4 (z_hi: 2, z_lo: 2; z = z_hi * 2 + z_lo), core: 2. Of those that a mesh axis runs over, the one named last changes fastest.
Arguments:
- image: bfloat16 [12288, 3072], P('patch', 'head'), may hold values from -6 to 6
- text: bfloat16 [256, 3072], P(None, 'head'), may hold values from -6 to 6
- text_len: int32 [1], replicated, may hold values from 64 to 256
- img_mod: float32 [3, 3072], replicated, may hold values from -4.2 to 4.2
- txt_mod: float32 [3, 3072], replicated, may hold values from -4.2 to 4.2
- img_qkv: bfloat16 [3072, 3, 3072], P(None, None, 'head'), may hold values from -0.109375 to 0.109375
- txt_qkv: bfloat16 [3072, 3, 3072], P(None, None, 'head'), may hold values from -0.109375 to 0.109375
- img_proj: bfloat16 [3072, 3072], P('head'), may hold values from -0.109375 to 0.109375
- txt_proj: bfloat16 [3072, 3072], P('head'), may hold values from -0.109375 to 0.109375
- img_gain: float32 [2, 128], replicated, may hold values from 1 to 2.5
- txt_gain: float32 [2, 128], replicated, may hold values from 1 to 2.5
- stale_kv: bfloat16 [2, 12288, 3072], P(None, 'patch', 'head'), may hold values from -2.5 to 2.5
Outputs:
- img_out: bfloat16 [12288, 3072], P('patch', 'head')
- txt_out: bfloat16 [256, 3072], P(None, 'head')
All inputs are finite; a program needn't handle non-finite values.
Results may differ from a plain program's by a relative error of at most 0.018.
Values may be sent and summed in bfloat16 or wider, within the bound.
No kernel may reach another device: no remote copies, remote signals or barrier semaphores. Data moves between devices by JAX's collectives and lax.ppermute only.
A program may use at most 128 MiB of HBM per device.

v0:
```python
import functools
import math

import jax
import jax.numpy as jnp
from jax import lax
from jax.experimental import pallas as pl
from jax.experimental.pallas import tpu as pltpu
from jax.sharding import PartitionSpec as P

EPS_NORM = 1e-06
BF = jnp.bfloat16
F32 = jnp.float32
VMEM = 56 * 2**20
NX, NY = 4, 4
TINY = pl.CostEstimate(flops=1, bytes_accessed=1, transcendentals=0)


def cost(us):
    return pl.CostEstimate(flops=int(us * 1.15e9), bytes_accessed=1, transcendentals=0)


def patch_perm(dz, dx, dc):
    return [
        ((z * NX + x) * 2 + c, ((z ^ dz) * NX + (x + dx) % NX) * 2 + (c ^ dc))
        for z in range(2)
        for x in range(NX)
        for c in range(2)
    ]


def head_perm(dz, dy):
    return [(z * NY + y, (z ^ dz) * NY + (y + dy) % NY) for z in range(2) for y in range(NY)]


def send_patch(x, dz=0, dx=0, dc=0):
    return lax.ppermute(x, "patch", patch_perm(dz, dx, dc))


def send_head(x, dz=0, dy=0):
    return lax.ppermute(x, "head", head_perm(dz, dy))


def in_hbm(x):
    return pltpu.with_memory_space_constraint(x, pltpu.HBM)


def after(x, *deps):
    return lax.optimization_barrier((x,) + deps)[0]


def lane_sum(parts, hd):
    acc = None
    for p in parts:
        for c in range(0, p.shape[1], hd):
            piece = p[:, c : c + hd]
            acc = piece if acc is None else acc + piece
    return jnp.sum(acc, axis=-1, keepdims=True)


def moments(vals, hd):
    mean = lane_sum(vals, hd) * (1.0 / sum(v.shape[1] for v in vals))
    vals = [v - mean for v in vals]
    return mean, vals, lane_sum([v * v for v in vals], hd)


def rms_heads(mixed, gain):
    hd = gain.shape[1]
    heads = []
    for c in range(0, mixed.shape[1], hd):
        v = mixed[:, c : c + hd]
        rms = lax.rsqrt(jnp.mean(v * v, axis=-1, keepdims=True) + EPS_NORM)
        heads.append((v * rms * gain).astype(BF))
    return jnp.concatenate(heads, axis=1)


def query_scale(hd):
    return hd ** (-0.5) * math.log2(math.e)


def weight_copies(idx_ref, w_ref, w_buf, sem, first):
    width = w_ref.shape[2]
    return [
        pltpu.make_async_copy(
            w_ref.at[p, pl.ds(pl.multiple_of(idx_ref[first + n] * width, width), width)],
            w_buf.at[pl.ds(n * width, width), pl.ds(p * width, width)],
            sem.at[p, n],
        )
        for n in range(sem.shape[1])
        for p in range(3)
    ]


def early_kernel(idx_ref, *refs, blocks, rows):
    x_refs = refs[:blocks]
    w_ref, mod_ref, acc_ref, stat_ref, x_buf, w_buf, mod_buf, x_sem, w_sem = refs[blocks:]
    width = x_buf.shape[2]
    hd = stat_ref.shape[2]
    x_copies = [
        pltpu.make_async_copy(x_refs[n].at[pl.ds(0, rows)], x_buf.at[n], x_sem.at[n]) for n in range(blocks)
    ]
    w_copies = weight_copies(idx_ref, w_ref, w_buf, w_sem, 0)
    for copy in x_copies + w_copies:
        copy.start()
    for n in range(blocks):
        cols = slice(n * width, (n + 1) * width)
        m = mod_ref[idx_ref[n]]
        scale, shift = 1.0 + m[1:2], m[0:1]
        high, low = [v.astype(BF) for v in (scale, shift)]
        pieces = [high, (scale - high.astype(F32)).astype(BF), low, (shift - low.astype(F32)).astype(BF)]
        tail = mod_buf.shape[0] - rows - len(pieces)
        mod_buf[rows:, cols] = jnp.concatenate(pieces + [jnp.zeros((tail, width), BF)], axis=0)
    for copy in x_copies:
        copy.wait()
    for o in range(0, rows, 16):
        mean, vals, square = moments([x_buf[n, o : o + 16].astype(F32) for n in range(blocks)], hd)
        inverse = lax.rsqrt(square * (1.0 / (blocks * width)) + EPS_NORM)
        stat_ref[0, o : o + 16] = jnp.broadcast_to(mean, (16, hd))
        stat_ref[1, o : o + 16] = jnp.broadcast_to(square, (16, hd))
        for n, v in enumerate(vals):
            out = v * inverse * (1.0 + mod_ref[idx_ref[n]][1:2])
            mod_buf[o : o + 16, n * width : (n + 1) * width] = out.astype(BF)
    for copy in w_copies:
        copy.wait()
    acc_ref[...] = jnp.dot(mod_buf[...], w_buf[...], preferred_element_type=F32)


def late_kernel(idx_ref, *refs, first, tile, scale):
    lone = len(refs) - 15
    x_refs = list(refs[:lone]) + [refs[lone].at[0], refs[lone].at[1]]
    w_ref, acc_hbm, stat_ref, mod_ref, gain_ref, q_ref, kv_ref = refs[lone + 1 : lone + 8]
    x_buf, w_buf, acc_ref, mod_buf, x_sem, w_sem, acc_sem = refs[lone + 8 :]
    blocks, rows, width = x_buf.shape
    hd = gain_ref.shape[1]
    tiles = rows // tile
    n_first, n_last = first * width, blocks * width
    x_copies = [
        [
            pltpu.make_async_copy(
                x_refs[n].at[pl.ds(t * tile, tile)], x_buf.at[n, pl.ds(t * tile, tile)], x_sem.at[t, n]
            )
            for n in range(blocks)
        ]
        for t in range(tiles)
    ]
    w_copies = weight_copies(idx_ref, w_ref, w_buf, w_sem, first)
    acc_copy = pltpu.make_async_copy(acc_hbm, acc_ref, acc_sem)
    for copy in x_copies[0] + w_copies + [acc_copy] + sum(x_copies[1:], []):
        copy.start()
    factors = {}

    def normalise(t):
        for copy in x_copies[t]:
            copy.wait()
        ratios, shifts = [], []
        for o in range(t * tile, (t + 1) * tile, 16):
            mean, vals, square = moments([x_buf[n, o : o + 16].astype(F32) for n in range(blocks)], hd)
            mean0 = stat_ref[0, o : o + 16, 0:1]
            square0 = stat_ref[1, o : o + 16, 0:1]
            gap = mean0 - mean
            total = square + square0 + gap * gap * (n_first * n_last / (n_first + n_last))
            inverse = lax.rsqrt(total * (1.0 / (n_first + n_last)) + EPS_NORM)
            center = mean + gap * (n_first / (n_first + n_last))
            ratios.append(inverse * jnp.sqrt(square0 * (1.0 / n_first) + EPS_NORM))
            shifts.append((mean0 - center) * inverse)
            for n, v in enumerate(vals):
                m = mod_ref[idx_ref[first + n]]
                out = (v + (mean - center)) * inverse * (1.0 + m[1:2]) + m[0:1]
                mod_buf[o : o + 16, n * width : (n + 1) * width] = out.astype(BF)
        factors[t] = (jnp.concatenate(ratios, axis=0), jnp.concatenate(shifts, axis=0))

    normalise(0)
    for copy in w_copies + [acc_copy]:
        copy.wait()
    scales = acc_ref[rows : rows + 1] + acc_ref[rows + 1 : rows + 2]
    offset = acc_ref[rows + 2 : rows + 3] + acc_ref[rows + 3 : rows + 4]
    for t in range(tiles):
        part = slice(t * tile, (t + 1) * tile)
        mixed = jnp.dot(mod_buf[part], w_buf[...], preferred_element_type=F32)
        if t + 1 < tiles:
            normalise(t + 1)
        ratio, shift = factors[t]
        mixed = mixed + acc_ref[part] * ratio + shift * scales + offset
        q_ref[part] = rms_heads(mixed[:, :width], gain_ref[0:1] * scale)
        kv_ref[0, part] = rms_heads(mixed[:, width : 2 * width], gain_ref[1:2])
        kv_ref[1, part] = mixed[:, 2 * width :].astype(BF)


def early_qkv(idx, x_list, w, mod, rows):
    width = x_list[0].shape[1]
    n = len(x_list)
    hd = 128
    hbm = pl.BlockSpec(memory_space=pltpu.HBM)
    vmem = pl.BlockSpec(memory_space=pltpu.VMEM)
    return pl.pallas_call(
        functools.partial(early_kernel, blocks=n, rows=rows),
        in_specs=[pl.BlockSpec(memory_space=pltpu.SMEM)] + [hbm] * (n + 1) + [vmem],
        out_specs=[vmem] * 2,
        out_shape=[
            jax.ShapeDtypeStruct((rows + 16, 3 * width), F32),
            jax.ShapeDtypeStruct((2, rows, hd), F32),
        ],
        scratch_shapes=[
            pltpu.VMEM((n, rows, width), BF),
            pltpu.VMEM((n * width, 3 * width), BF),
            pltpu.VMEM((rows + 16, n * width), BF),
            pltpu.SemaphoreType.DMA((n,)),
            pltpu.SemaphoreType.DMA((3, n)),
        ],
        compiler_params=pltpu.CompilerParams(vmem_limit_bytes=VMEM),
        cost_estimate=TINY,
        name="early_qkv",
    )(idx, *x_list, w, mod)


def late_qkv(idx, x_list, w, acc, stat, mod, gain):
    rows, width = stat.shape[1], x_list[0].shape[1]
    n = len(x_list) + 1
    first = mod.shape[0] - n
    tile = rows // 2
    hbm = pl.BlockSpec(memory_space=pltpu.HBM)
    vmem = pl.BlockSpec(memory_space=pltpu.VMEM)
    return pl.pallas_call(
        functools.partial(
            late_kernel, first=first, tile=tile, scale=query_scale(gain.shape[1])
        ),
        in_specs=[pl.BlockSpec(memory_space=pltpu.SMEM)] + [hbm] * (n + 1) + [vmem] * 3,
        out_specs=[vmem] * 2,
        out_shape=[
            jax.ShapeDtypeStruct((rows, width), BF),
            jax.ShapeDtypeStruct((2, rows, width), BF),
        ],
        scratch_shapes=[
            pltpu.VMEM((n, rows, width), BF),
            pltpu.VMEM((n * width, 3 * width), BF),
            pltpu.VMEM(acc.shape, F32),
            pltpu.VMEM((rows, n * width), BF),
            pltpu.SemaphoreType.DMA((2, n)),
            pltpu.SemaphoreType.DMA((3, n)),
            pltpu.SemaphoreType.DMA,
        ],
        compiler_params=pltpu.CompilerParams(vmem_limit_bytes=VMEM),
        cost_estimate=TINY,
        name="late_qkv",
    )(idx, *x_list, w, acc, stat, mod, gain)


def text_qkv_kernel(idx_ref, *refs, blocks, scale):
    x_refs = list(refs[: blocks - 2]) + [refs[blocks - 2].at[0], refs[blocks - 2].at[1]]
    w_ref, mod_ref, gain_ref, out_ref, mod_buf = refs[blocks - 1 :]
    width = x_refs[0].shape[1]
    vals = [r[...].astype(F32) for r in x_refs]
    _, vals, square = moments(vals, gain_ref.shape[1])
    inverse = lax.rsqrt(square * (1.0 / (blocks * width)) + EPS_NORM)
    for n, v in enumerate(vals):
        m = mod_ref[idx_ref[n]]
        out = (v * inverse * (1.0 + m[1:2]) + m[0:1]).astype(BF)
        mod_buf[:, pl.ds(pl.multiple_of(idx_ref[n] * width, 128), width)] = out
    mixed = [jnp.dot(mod_buf[...], w_ref[p], preferred_element_type=F32) for p in range(3)]
    out_ref[:, :width] = rms_heads(mixed[0], gain_ref[0:1] * scale)
    out_ref[:, width : 2 * width] = rms_heads(mixed[1], gain_ref[1:2])
    out_ref[:, 2 * width :] = mixed[2].astype(BF)


def text_qkv(idx, x_list, w, mod, gain, rows):
    total, width = x_list[0].shape
    n = len(x_list) + 1
    last = total // rows - 1
    vmem = pl.BlockSpec(memory_space=pltpu.VMEM)
    return pl.pallas_call(
        functools.partial(text_qkv_kernel, blocks=n, scale=query_scale(gain.shape[1])),
        grid=(1,),
        in_specs=[pl.BlockSpec(memory_space=pltpu.SMEM)]
        + [pl.BlockSpec((rows, width), lambda i: (last, 0))] * (n - 2)
        + [pl.BlockSpec((2, rows, width), lambda i: (0, last, 0))]
        + [vmem] * 3,
        out_specs=vmem,
        out_shape=jax.ShapeDtypeStruct((rows, 3 * width), BF),
        scratch_shapes=[pltpu.VMEM((rows, n * width), BF)],
        compiler_params=pltpu.CompilerParams(vmem_limit_bytes=24 * 2**20),
        cost_estimate=cost(2),
        name="text_qkv",
    )(idx, *[in_hbm(x) for x in x_list], w, mod, gain)


def one(q, k, v, valid=None):
    s = lax.dot_general(q, k, (((1,), (1,)), ((), ())), preferred_element_type=F32)
    e = jnp.exp2(s)
    if valid is not None:
        e = jnp.where(lax.broadcasted_iota(jnp.int32, e.shape, 1) < valid, e, 0.0)
    hd = v.shape[1]
    wide = jnp.concatenate([v, jnp.ones_like(v)], axis=1)
    both = jnp.dot(e.astype(BF), wide, preferred_element_type=F32)
    return both[:, :hd], both[:, hd:]


def att_kernel(pos_ref, *refs, plan, n_q, n_kv, text, acc, packed):
    refs = list(refs)
    length = refs.pop(0) if text else None
    qs = [refs.pop(0) for _ in range(n_q)]
    kvs = [refs.pop(0) for _ in range(n_kv)]
    txt = [refs.pop(0) for _ in range(2)] if text else None
    accs = [refs.pop(0) for _ in range(2 * n_q)] if acc else None
    for i in range(n_q):
        num = accs[2 * i][...] if acc else None
        den = accs[2 * i + 1][...] if acc else None
        q = qs[i][...]
        parts = [(kvs[j].at[0], kvs[j].at[1], None) for j in plan[i]]
        if text and i == 0:
            parts.append((txt[0], txt[1], length[0]))
        for k_ref, v_ref, valid in parts:
            n, d = one(q, k_ref[...], v_ref[...], valid)
            num = n if num is None else num + n
            den = d if den is None else den + d
        if i in packed:
            out = refs.pop(0)
            out[0] = num.astype(BF)
            out[1] = den.astype(BF)
        else:
            refs.pop(0)[...] = num
            refs.pop(0)[...] = den


def attention(pos, qs, kvs, plan, text=None, acc=None, packed=(), rows=None, chunk=0, width=None, name="att"):
    width = qs[0].shape[1] if width is None else width
    rows = qs[0].shape[0] if rows is None else rows
    hd = 128
    heads = width // hd
    n_q = len(qs)
    args, specs = [], []
    if text is not None:
        args.append(text[0])
        specs.append(pl.BlockSpec(memory_space=pltpu.SMEM))
    q_spec = pl.BlockSpec((rows, hd), lambda h, p: (chunk, h))
    out_spec = pl.BlockSpec((rows, hd), lambda h, p: (0, h))
    for q in qs:
        args.append(q)
        specs.append(q_spec)
    keys = 0
    for kv in kvs:
        keys = kv.shape[1]
        specs.append(pl.BlockSpec((2, keys, hd), lambda h, p: (0, 0, h)))
        args.append(kv)
    if text is not None:
        tk = text[1]
        args += [tk, tk]
        specs.append(pl.BlockSpec((tk.shape[0], hd), lambda h, p: (0, heads + h)))
        specs.append(pl.BlockSpec((tk.shape[0], hd), lambda h, p: (0, 2 * heads + h)))
    if acc is not None:
        args += list(acc)
        specs += [q_spec] * len(acc)
    outs, out_specs = [], []
    for i in range(n_q):
        if i in packed:
            outs.append(jax.ShapeDtypeStruct((2, rows, width), BF))
            out_specs.append(pl.BlockSpec((2, rows, hd), lambda h, p: (0, 0, h)))
        else:
            outs += [jax.ShapeDtypeStruct((rows, width), F32)] * 2
            out_specs += [out_spec] * 2
    blocks = sum(len(p) for p in plan)
    return pl.pallas_call(
        functools.partial(
            att_kernel, plan=plan, n_q=n_q, n_kv=len(kvs), text=text is not None, acc=acc is not None, packed=packed
        ),
        grid_spec=pltpu.PrefetchScalarGridSpec(
            num_scalar_prefetch=1, grid=(heads,), in_specs=specs, out_specs=out_specs
        ),
        out_shape=outs,
        compiler_params=pltpu.CompilerParams(vmem_limit_bytes=VMEM),
        cost_estimate=pl.CostEstimate(
            flops=14 * rows * keys * width * blocks, bytes_accessed=1, transcendentals=0
        ),
        name=name,
    )(pos, *args)


def text_att_kernel(q_ref, kv_ref, out_ref):
    n_patch, _, rows, width = out_ref.shape
    hd = 128
    for h in range(width // hd):
        cols = slice(h * hd, (h + 1) * hd)
        num, den = one(q_ref[:, cols], kv_ref[0, :, cols], kv_ref[1, :, cols])
        out_ref[:, 0, :, cols] = num.astype(BF).reshape(n_patch, rows, hd)
        out_ref[:, 1, :, cols] = den.astype(BF).reshape(n_patch, rows, hd)


def text_attention(txt, kv, n_patch):
    rows = txt.shape[0]
    width = kv.shape[2]
    return pl.pallas_call(
        text_att_kernel,
        grid=(1,),
        in_specs=[pl.BlockSpec((rows, width), lambda i: (0, 0)), pl.BlockSpec(kv.shape, lambda i: (0, 0, 0))],
        out_specs=pl.BlockSpec((n_patch, 2, rows // n_patch, width), lambda i: (0, 0, 0, 0)),
        out_shape=jax.ShapeDtypeStruct((n_patch, 2, rows // n_patch, width), BF),
        compiler_params=pltpu.CompilerParams(vmem_limit_bytes=VMEM),
        cost_estimate=cost(3),
        name="text_attention",
    )(txt, kv)


def text_keys(q_ref, txt_ref, len_ref, h):
    hd = 128
    width = q_ref.shape[1]
    at = h * hd
    k = txt_ref[:, width + at : width + at + hd]
    v = txt_ref[:, 2 * width + at : 2 * width + at + hd]
    return one(q_ref[:, at : at + hd], k, v, len_ref[0])


def image_quotient(len_ref, q_ref, txt_ref, num_ref, den_ref, got_ref, attn_ref):
    hd = 128
    rows = num_ref.shape[0]
    for h in range(num_ref.shape[1] // hd):
        cols = slice(h * hd, (h + 1) * hd)
        n, d = text_keys(q_ref, txt_ref, len_ref, h)
        num = n + num_ref[:, cols] + got_ref[0, :, cols].astype(F32)
        den = d + den_ref[:, cols] + got_ref[1, :, cols].astype(F32)
        attn_ref[0:rows, cols] = (num / den).astype(BF)


def quotient(text_len, q, txt, num, den, got):
    vmem = pl.BlockSpec(memory_space=pltpu.VMEM)
    return pl.pallas_call(
        image_quotient,
        in_specs=[pl.BlockSpec(memory_space=pltpu.SMEM)] + [vmem] * 5,
        out_specs=vmem,
        out_shape=jax.ShapeDtypeStruct(q.shape, BF),
        compiler_params=pltpu.CompilerParams(vmem_limit_bytes=VMEM),
        cost_estimate=cost(4),
        name="quotient",
    )(text_len, q, txt, num, den, got)


def text_quotient_kernel(len_ref, sum_ref, q_ref, txt_ref, proj_ref, out_ref):
    rows, width = q_ref.shape
    hd = 128
    parts = []
    for h in range(width // hd):
        cols = slice(h * hd, (h + 1) * hd)
        n, d = text_keys(q_ref, txt_ref, len_ref, h)
        num = n + jnp.sum(sum_ref[:, 0, :, cols].astype(F32), axis=0)
        den = d + jnp.sum(sum_ref[:, 1, :, cols].astype(F32), axis=0)
        parts.append((num / den).astype(BF))
    attn = jnp.concatenate(parts, axis=1)
    part = jnp.dot(attn, proj_ref[...], preferred_element_type=F32).astype(BF)
    for j in range(out_ref.shape[0]):
        out_ref[j] = part[:, j * width : (j + 1) * width]


def text_quotient(text_len, sums, q, txt, proj, n_head):
    vmem = pl.BlockSpec(memory_space=pltpu.VMEM)
    return pl.pallas_call(
        text_quotient_kernel,
        in_specs=[pl.BlockSpec(memory_space=pltpu.SMEM)] + [vmem] * 4,
        out_specs=vmem,
        out_shape=jax.ShapeDtypeStruct((n_head,) + q.shape, BF),
        compiler_params=pltpu.CompilerParams(vmem_limit_bytes=VMEM),
        cost_estimate=cost(4),
        name="text_quotient",
    )(text_len, sums, q, txt, proj)


def proj_kernel(pos_ref, mine_ref, got_ref, w_ref, wz_ref, *refs):
    outs = refs[:NY]
    w_buf, sem = refs[NY:]
    width = mine_ref.shape[1]
    zh, y = pos_ref[0], pos_ref[1]
    order = (2, 1, 3, 0)

    def copies(d):
        block = lax.rem(y + d, NY)
        pairs = ((w_ref, zh * NY + block), (wz_ref, block))
        return [
            pltpu.make_async_copy(
                ref.at[:, pl.ds(pl.multiple_of(at * width, 128), width)],
                w_buf.at[d, pl.ds(i * width, width)],
                sem.at[d, i],
            )
            for i, (ref, at) in enumerate(pairs)
        ]

    for d in order:
        for copy in copies(d):
            copy.start()
    both = jnp.concatenate([mine_ref[...], got_ref[...]], axis=1)
    for d in order:
        for copy in copies(d):
            copy.wait()
        outs[d][...] = jnp.dot(both, w_buf[d], preferred_element_type=F32).astype(BF)


def project(pos, mine, got, w, wz):
    width = mine.shape[1]
    spec = pl.BlockSpec(memory_space=pltpu.VMEM)
    hbm = pl.BlockSpec(memory_space=pltpu.HBM)
    return pl.pallas_call(
        proj_kernel,
        in_specs=[pl.BlockSpec(memory_space=pltpu.SMEM)] + [spec] * 2 + [hbm] * 2,
        out_specs=[spec] * NY,
        out_shape=[jax.ShapeDtypeStruct(mine.shape, BF)] * NY,
        scratch_shapes=[
            pltpu.VMEM((NY, 2 * width, width), BF),
            pltpu.SemaphoreType.DMA((NY, 2)),
        ],
        compiler_params=pltpu.CompilerParams(vmem_limit_bytes=VMEM),
        cost_estimate=cost(6),
        name="project",
    )(pos, mine, got, w, wz)


def exchange(parts):
    total = parts[0].astype(F32)
    for d in range(1, NY):
        total = total + send_head(parts[d], dy=d).astype(F32)
    return total


def shards(
    image,
    text,
    text_len,
    img_mod,
    txt_mod,
    img_qkv,
    txt_qkv,
    img_proj,
    txt_proj,
    img_gain,
    txt_gain,
    stale_kv,
):
    n_head = lax.axis_size("head")
    n_patch = lax.axis_size("patch")
    me_h = lax.axis_index("head")
    me_p = lax.axis_index("patch")
    zh, y = me_h // NY, me_h % NY
    group, width = image.shape
    txt_total = text.shape[0]
    t_rows = txt_total // n_patch

    pos = jnp.stack([zh, y]).astype(jnp.int32)

    t_own = lax.dynamic_slice_in_dim(text, me_p * t_rows, t_rows, 0)
    rows = jnp.concatenate([image, t_own], axis=0)
    i_z = send_head(rows, dz=1)
    i_m = send_head(rows, dy=1)
    i_p = send_head(rows, dy=-1)
    kv_m = send_patch(stale_kv, dx=1)
    part_z = lax.dynamic_slice_in_dim(img_proj, (1 - zh) * NY * width, NY * width, 1)
    near = after(i_z, i_m, i_p, part_z)
    ahead = send_head(jnp.stack([i_m, near]), dy=1)
    iz_p = send_head(near, dy=-1)
    mod_i = img_mod.reshape(3, n_head, width).transpose(1, 0, 2)
    mod_t = txt_mod.reshape(3, n_head, width).transpose(1, 0, 2)
    ring = (y + jnp.array([0, 0, NY - 1, 1, 1, 2, 2, NY - 1])) % NY
    side = (zh + jnp.array([0, 1, 0, 0, 1, 1, 0, 1])) % 2
    idx = (side * NY + ring).astype(jnp.int32)
    w_i = img_qkv.transpose(1, 0, 2)
    iz_2 = send_head(iz_p, dy=-1)
    acc, stat = early_qkv(after(idx, kv_m, iz_p), [rows, near, i_m, i_p], w_i, mod_i, group)
    later = after(stale_kv, iz_p)
    kv_z = send_patch(later, dz=1)
    kv_p = send_patch(later, dx=-1)
    kv_2 = send_patch(kv_m, dx=1)
    kvz_m = send_patch(kv_z, dx=1)
    kvz_p = send_patch(kv_z, dx=-1)
    kvz_2 = send_patch(kv_2, dz=1)
    proj_z = send_head(after(part_z, kv_z), dz=1)
    q, kv = late_qkv(idx, [iz_p, iz_2, ahead], w_i, acc, stat, mod_i, img_gain)
    x_list = [rows, near, i_m, i_p, iz_p, iz_2, ahead]
    q_c = send_patch(q, dc=1)
    t_pack = text_qkv(after(idx, q), x_list, txt_qkv.transpose(1, 0, 2), mod_t, txt_gain, t_rows)
    t_q = t_pack[:, :width]
    txt = lax.all_to_all(
        jnp.broadcast_to(t_pack[None], (n_patch,) + t_pack.shape), "patch", 0, 0
    ).reshape(txt_total, 3 * width)

    both = attention(
        after(pos, t_pack), [q, q_c], [kv, stale_kv, kv_m, kv_p], [[0, 2, 3], [1, 2, 3]], name="att_near"
    )
    both = attention(pos, [q, q_c], [kv_2, kv_z], [[0, 1]] * 2, acc=both, name="att_mid")
    t_sums = text_attention(after(txt, both[0]), kv, n_patch)
    t_got = lax.all_to_all(t_sums, "patch", 0, 0)
    num, den, part_c = attention(
        after(pos, t_sums),
        [q, q_c],
        [kvz_m, kvz_p, kvz_2],
        [[0, 1, 2]] * 2,
        acc=both,
        packed=(1,),
        name="att_last",
    )
    got_c = send_patch(part_c, dc=1)
    attn = quotient(text_len, q, txt, num, den, after(got_c, proj_z))
    from_z = send_head(attn, dz=1)
    t_proj = text_quotient(text_len, after(t_got, attn), t_q, txt, txt_proj, n_head)
    outs = project(pos, attn, from_z, img_proj, proj_z)
    img_sum = exchange(outs)
    column = me_h * width
    img_gate = lax.dynamic_slice_in_dim(img_mod[2], column, width)
    img_out = (image.astype(F32) + img_gate * img_sum).astype(BF)
    t_sum = lax.all_to_all(t_proj, "head", 0, 0).astype(F32).sum(axis=0)
    txt_gate = lax.dynamic_slice_in_dim(txt_mod[2], column, width)
    t_out = (t_own.astype(F32) + txt_gate * t_sum).astype(BF)
    txt_out = lax.all_to_all(
        jnp.broadcast_to(t_out[None], (n_patch,) + t_out.shape), "patch", 0, 0
    ).reshape(txt_total, width)
    return (img_out, txt_out)


def solution(mesh):
    in_specs = (
        P("patch", "head"),
        P(None, "head"),
        P(),
        P(),
        P(),
        P(None, None, "head"),
        P(None, None, "head"),
        P("head", None),
        P("head", None),
        P(),
        P(),
        P(None, "patch", "head"),
    )
    out_specs = (P("patch", "head"), P(None, "head"))
    return jax.shard_map(shards, mesh=mesh, in_specs=in_specs, out_specs=out_specs, check_vma=False)
```

profile of v0, /device:TPU:0, one launch (start us, length us, event | category | flops | bytes accessed | tf_op | source)
XLA Modules:
  0.0 197.4 jit_solution(3500574815346623075)
XLA Ops:
  2.5 1.7 collective-permute-start.1
  5.8 4.0 %collective-permute-start = (bf16[784,384]{1,0:T(8,128)(2,1)S(1)}, bf16[784,384]{1,0:T(8,128)(2,1)S(1)}, u32[]{:S(2)}, u32[]{:S(2)}) collective-permute-start(bf16[784,384]{1,0:T(8,128)(2,1)S(1)} %pad_maximum_fusion.1.refs_0_), channel_id=1, source_target_pairs={{0,4},{1,5},{2,6},{3,7},{4,0},{5,1},{6,2},{7,3},{8,12},{9,13},{10,... | collective-permute-start | bytes 1806344 | tf_op jit(solution)/shard_map/ppermute | solution.py:41
  11.2 2.4 %constant_dynamic-slice_fusion = bf16[384,1536]{1,0:T(8,128)(2,1)} fusion(bf16[384,3072]{1,0:T(8,128)(2,1)} %w_ref.1, s32[]{:T(128)S(6)} %select_n.37), kind=kLoop, calls=%fused_computation.13 | loop fusion | bytes 2359300 | tf_op jit(solution)/shard_map/dynamic_slice | solution.py:550
  13.6 5.6 %collective-permute-done.1.refs_2_ = bf16[784,384]{1,0:T(8,128)(2,1)S(1)} collective-permute-done((bf16[784,384]{1,0:T(8,128)(2,1)S(1)}, bf16[784,384]{1,0:T(8,128)(2,1)S(1)}, u32[]{:S(2)}, u32[]{:S(2)}) %collective-permute-start.1) | collective-permute-done | bytes 602144 | tf_op jit(solution)/shard_map/ppermute | solution.py:41
  19.3 3.7 %collective-permute-done.refs_1_ = bf16[784,384]{1,0:T(8,128)(2,1)S(1)} collective-permute-done((bf16[784,384]{1,0:T(8,128)(2,1)S(1)}, bf16[784,384]{1,0:T(8,128)(2,1)S(1)}, u32[]{:S(2)}, u32[]{:S(2)}) %collective-permute-start) | collective-permute-done | bytes 602144 | tf_op jit(solution)/shard_map/ppermute | solution.py:41
  26.1 11.1 %collective-permute-done.3.refs_0_.refs_4_ = bf16[784,384]{1,0:T(8,128)(2,1)S(1)} collective-permute-done((bf16[784,384]{1,0:T(8,128)(2,1)S(1)}, bf16[784,384]{1,0:T(8,128)(2,1)S(1)}, u32[]{:S(2)}, u32[]{:S(2)}) %collective-permute-start.3) | collective-permute-done | bytes 602144 | tf_op jit(solution)/shard_map/ppermute | solution.py:41
  37.2 2.7 %collective-permute-start.4 = (bf16[784,384]{1,0:T(8,128)(2,1)S(1)}, bf16[784,384]{1,0:T(8,128)(2,1)S(1)}, u32[]{:S(2)}, u32[]{:S(2)}) collective-permute-start(bf16[784,384]{1,0:T(8,128)(2,1)S(1)} %collective-permute-done.3.refs_0_.refs_4_), channel_id=1, source_target_pairs={{0,3},{1,0},{2,1},{3,2},{4,7},{5,4},{6,5},{7,6},{8,11},{9,8},{10,9... | collective-permute-start | bytes 1806344 | tf_op jit(solution)/shard_map/ppermute | solution.py:41
  42.4 1.9 collective-permute-start.10
  44.9 10.1 %early_qkv.1 = (f32[784,1152]{1,0:T(8,128)}, f32[2,768,128]{2,1,0:T(8,128)}) custom-call(s32[8]{0:T(128)} %fusion.idx_ref, bf16[784,384]{1,0:T(8,128)(2,1)} %copy-done.3, bf16[784,384]{1,0:T(8,128)(2,1)} %copy-done.5, bf16[784,384]{1,0:T(8,128)(2,1)} %copy-done.4, bf16[784,384]{1,0:T(8,128)(2,1)} %copy-done.7, bf16[3,3072,384]{2,1,0:T(8,128)(2,1)} %bitcast.18, ...), custom_call_target="tpu_custom_call" | custom-call | flops 1 | bytes 1 | tf_op jit(solution)/shard_map/early_qkv/pallas_call | solution.py:195
  56.2 11.7 %late_qkv.1 = (bf16[768,384]{1,0:T(8,128)(2,1)}, bf16[2,768,384]{2,1,0:T(8,128)(2,1)}) custom-call(s32[8]{0:T(128)} %fusion.idx_ref, bf16[784,384]{1,0:T(8,128)(2,1)} %copy-done.8, bf16[784,384]{1,0:T(8,128)(2,1)} %copy-done.9, bf16[2,784,384]{2,1,0:T(8,128)(2,1)} %copy-done.6, bf16[3,3072,384]{2,1,0:T(8,128)(2,1)} %bitcast.19, ...), custom_call_target="tpu_custom_call" | custom-call | flops 1 | bytes 1 | tf_op jit(solution)/shard_map/late_qkv/pallas_call | solution.py:223
  68.7 2.1 %text_qkv.1 = bf16[16,1152]{1,0:T(8,128)(2,1)S(1)} custom-call(s32[8]{0:T(128)S(1)} %copy-done.1, bf16[784,384]{1,0:T(8,128)(2,1)} %copy-done.3, bf16[784,384]{1,0:T(8,128)(2,1)} %copy-done.5, bf16[784,384]{1,0:T(8,128)(2,1)} %copy-done.4, bf16[784,384]{1,0:T(8,128)(2,1)} %copy-done.7, bf16[784,384]{1,0:T(8,128)(2,1)} %copy-done.8, ...), custom_call_target="tpu_custom_call" | custom-call | flops 2300000000 | bytes 1 | tf_op jit(solution)/shard_map/text_qkv/pallas_call | solution.py:270
  71.7 3.9 %all-to-all-start = ((bf16[16,16,1152]{2,1,0:T(8,128)(2,1)}), bf16[16,16,1152]{2,1,0:T(8,128)(2,1)S(1)}, u32[]{:S(2)}, u32[]{:S(2)}) async-start(bf16[16,16,1152]{2,1,0:T(8,128)(2,1)} %broadcast_in_dim.4), calls=%async_computation | async-start | bytes 1179648 | tf_op jit(solution)/shard_map/all_to_all | solution.py:575
  75.6 2.0 %collective-permute-start.13 = (bf16[2,768,384]{2,1,0:T(8,128)(2,1)}, bf16[2,768,384]{2,1,0:T(8,128)(2,1)}, u32[]{:S(2)}, u32[]{:S(2)}) collective-permute-start(bf16[2,768,384]{2,1,0:T(8,128)(2,1)} %collective-permute-done.8.refs_2_), channel_id=1, source_target_pairs={{0,64},{8,72},{16,80},{24,88},{32,96},{40,104},{48,112},{56,120},{... | collective-permute-start | bytes 3538952 | tf_op jit(solution)/shard_map/ppermute | solution.py:37
  77.6 3.5 %collective-permute-start.15 = (bf16[384,1536]{1,0:T(8,128)(2,1)S(1)}, bf16[384,1536]{1,0:T(8,128)(2,1)}, u32[]{:S(2)}, u32[]{:S(2)}) collective-permute-start(bf16[384,1536]{1,0:T(8,128)(2,1)S(1)} %copy-done.11), channel_id=1, source_target_pairs={{0,4},{1,5},{2,6},{3,7},{4,0},{5,1},{6,2},{7,3},{8,12},{9,13},{10,... | collective-permute-start | bytes 3538952 | tf_op jit(solution)/shard_map/ppermute | solution.py:41
  82.7 1.8 collective-permute-start.12
  85.3 15.1 %att_near.1 = (f32[768,384]{1,0:T(8,128)}, f32[768,384]{1,0:T(8,128)}, f32[768,384]{1,0:T(8,128)}, f32[768,384]{1,0:T(8,128)}) custom-call(s32[2]{0:T(128)} %pad_add_fusion.pos_ref, bf16[768,384]{1,0:T(8,128)(2,1)} %get-tuple-element.35.refs_0_.q_ref, bf16[768,384]{1,0:T(8,128)(2,1)} %copy-done.16, bf16[2,768,384]{2,1,0:T(8,128)(2,1)} %get-tuple-element.39.refs_2_.kv_ref, ...), custom_call_target="tpu_custom_call" | custom-call | flops 19025362944 | bytes 1 | tf_op jit(solution)/shard_map/att_near/pallas_call | solution.py:361
  100.4 11.8 %att_mid.1 = (f32[768,384]{1,0:T(8,128)}, f32[768,384]{1,0:T(8,128)}, f32[768,384]{1,0:T(8,128)}, f32[768,384]{1,0:T(8,128)}) custom-call(s32[2]{0:T(128)} %pad_add_fusion.pos_ref, bf16[768,384]{1,0:T(8,128)(2,1)} %get-tuple-element.35.refs_0_.q_ref, bf16[768,384]{1,0:T(8,128)(2,1)} %copy-done.16, bf16[2,768,384]{2,1,0:T(8,128)(2,1)} %collective-permute-done.8.refs_2_, ...), custom_call_target="tpu_custom_call" | custom-call | flops 12683575296 | bytes 1 | tf_op jit(solution)/shard_map/att_mid/pallas_call | solution.py:361
  113.0 3.0 %text_attention.1 = bf16[16,2,16,384]{3,2,1,0:T(8,128)(2,1)} custom-call(bf16[256,1152]{1,0:T(8,128)(2,1)} %bitcast.23, bf16[2,768,384]{2,1,0:T(8,128)(2,1)} %get-tuple-element.39.refs_2_.kv_ref), custom_call_target="tpu_custom_call" | custom-call | flops 3449999872 | bytes 1 | tf_op jit(solution)/shard_map/text_attention/pallas_call | solution.py:390
  116.1 15.4 %att_last.1 = (f32[768,384]{1,0:T(8,128)}, f32[768,384]{1,0:T(8,128)}, bf16[2,768,384]{2,1,0:T(8,128)(2,1)}) custom-call(s32[2]{0:T(128)} %pad_add_fusion.pos_ref, bf16[768,384]{1,0:T(8,128)(2,1)} %get-tuple-element.35.refs_0_.q_ref, bf16[768,384]{1,0:T(8,128)(2,1)} %copy-done.16, bf16[2,768,384]{2,1,0:T(8,128)(2,1)} %collective-permute-done.11.refs_2_, ...), custom_call_target="tpu_custom_call" | custom-call | flops 19025362944 | bytes 1 | tf_op jit(solution)/shard_map/att_last/pallas_call | solution.py:361
  132.3 3.6 %all-to-all-start.1 = ((bf16[16,2,16,384]{3,2,1,0:T(8,128)(2,1)}), bf16[16,2,16,384]{3,2,1,0:T(8,128)(2,1)S(1)}, u32[]{:S(2)}, u32[]{:S(2)}) async-start(bf16[16,2,16,384]{3,2,1,0:T(8,128)(2,1)} %text_attention.1), calls=%async_computation.1 | async-start | bytes 786432 | tf_op jit(solution)/shard_map/all_to_all | solution.py:584
  135.8 1.8 collective-permute-done.15.wz_ref
  137.6 4.1 %quotient.1.mine_ref = bf16[768,384]{1,0:T(8,128)(2,1)} custom-call(s32[1]{0:T(128)S(6)} %copy.17.len_ref, bf16[768,384]{1,0:T(8,128)(2,1)} %get-tuple-element.35.refs_0_.q_ref, bf16[256,1152]{1,0:T(8,128)(2,1)} %bitcast.24, f32[768,384]{1,0:T(8,128)} %get-tuple-element.50.num_ref, f32[768,384]{1,0:T(8,128)} %get-tuple-element.51.den_ref, ...), custom_call_target="tpu_custom_call" | custom-call | flops 4600000000 | bytes 1 | tf_op jit(solution)/shard_map/quotient/pallas_call | solution.py:424
  142.3 2.7 %all-to-all-done.1.sum_ref = bf16[16,2,16,384]{3,2,1,0:T(8,128)(2,1)S(1)} async-done(((bf16[16,2,16,384]{3,2,1,0:T(8,128)(2,1)}), bf16[16,2,16,384]{3,2,1,0:T(8,128)(2,1)S(1)}, u32[]{:S(2)}, u32[]{:S(2)}) %all-to-all-start.1) | async-done | bytes 393248 | tf_op jit(solution)/shard_map/all_to_all | solution.py:584
  145.8 3.4 %text_quotient.1 = bf16[8,16,384]{2,1,0:T(8,128)(2,1)} custom-call(s32[1]{0:T(128)S(6)} %copy.17.len_ref, bf16[16,2,16,384]{3,2,1,0:T(8,128)(2,1)} %copy-done.13, bf16[16,384]{1,0:T(8,128)(2,1)} %slice.12.q_ref, bf16[256,1152]{1,0:T(8,128)(2,1)} %bitcast.25, bf16[384,3072]{1,0:T(8,128)(2,1)} %proj_ref.1), custom_call_target="tpu_custom_call" | custom-call | flops 4600000000 | bytes 1 | tf_op jit(solution)/shard_map/text_quotient/pallas_call | solution.py:453
  149.1 3.4 %all-to-all-start.2 = ((bf16[8,16,384]{2,1,0:T(8,128)(2,1)}), bf16[8,16,384]{2,1,0:T(8,128)(2,1)S(1)}, u32[]{:S(2)}, u32[]{:S(2)}) async-start(bf16[8,16,384]{2,1,0:T(8,128)(2,1)} %text_quotient.1), calls=%async_computation.2 | async-start | bytes 196608 | tf_op jit(solution)/shard_map/all_to_all | solution.py:603
  152.5 6.6 %collective-permute-done.16.got_ref = bf16[768,384]{1,0:T(8,128)(2,1)S(1)} collective-permute-done((bf16[768,384]{1,0:T(8,128)(2,1)}, bf16[768,384]{1,0:T(8,128)(2,1)S(1)}, u32[]{:S(2)}, u32[]{:S(2)}) %collective-permute-start.16) | collective-permute-done | bytes 589856 | tf_op jit(solution)/shard_map/ppermute | solution.py:41
  159.9 6.3 %project.1 = (bf16[768,384]{1,0:T(8,128)(2,1)}, bf16[768,384]{1,0:T(8,128)(2,1)}, bf16[768,384]{1,0:T(8,128)(2,1)}, bf16[768,384]{1,0:T(8,128)(2,1)}) custom-call(s32[2]{0:T(128)} %pad_add_fusion.pos_ref, bf16[768,384]{1,0:T(8,128)(2,1)} %quotient.1.mine_ref, bf16[768,384]{1,0:T(8,128)(2,1)} %copy-done.17, bf16[384,3072]{1,0:T(8,128)(2,1)} %w_ref.1, ...), custom_call_target="tpu_custom_call" | custom-call | flops 6899999744 | bytes 1 | tf_op jit(solution)/shard_map/project/pallas_call | solution.py:497
  166.8 2.7 %collective-permute-start.19 = (bf16[768,384]{1,0:T(8,128)(2,1)}, bf16[768,384]{1,0:T(8,128)(2,1)S(1)}, u32[]{:S(2)}, u32[]{:S(2)}) collective-permute-start(bf16[768,384]{1,0:T(8,128)(2,1)} %get-tuple-element.58), channel_id=1, source_target_pairs={{0,3},{1,0},{2,1},{3,2},{4,7},{5,4},{6,5},{7,6},{8,11},{9,8},{10,9... | collective-permute-start | bytes 1769480 | tf_op jit(solution)/shard_map/ppermute | solution.py:41
  171.0 5.0 %all-to-all-start.3 = ((bf16[16,16,384]{2,1,0:T(8,128)(2,1)}), bf16[16,16,384]{2,1,0:T(8,128)(2,1)S(1)}, u32[]{:S(2)}, u32[]{:S(2)}) async-start(bf16[16,16,384]{2,1,0:T(8,128)(2,1)} %broadcast_in_dim.5), calls=%async_computation.3 | async-start | bytes 393216 | tf_op jit(solution)/shard_map/all_to_all | solution.py:606
  176.9 6.3 %all-to-all-done.3 = bf16[16,16,384]{2,1,0:T(8,128)(2,1)S(1)} async-done(((bf16[16,16,384]{2,1,0:T(8,128)(2,1)}), bf16[16,16,384]{2,1,0:T(8,128)(2,1)S(1)}, u32[]{:S(2)}, u32[]{:S(2)}) %all-to-all-start.3) | async-done | bytes 196640 | tf_op jit(solution)/shard_map/all_to_all | solution.py:606
  183.2 10.7 %collective-permute-done.17 = bf16[768,384]{1,0:T(8,128)(2,1)S(1)} collective-permute-done((bf16[768,384]{1,0:T(8,128)(2,1)}, bf16[768,384]{1,0:T(8,128)(2,1)S(1)}, u32[]{:S(2)}, u32[]{:S(2)}) %collective-permute-start.17) | collective-permute-done | bytes 589856 | tf_op jit(solution)/shard_map/ppermute | solution.py:41
  194.5 2.3 %add_convert_fusion = bf16[768,384]{1,0:T(8,128)(2,1)} fusion(bf16[768,384]{1,0:T(8,128)(2,1)S(1)} %collective-permute-done.19, bf16[768,384]{1,0:T(8,128)(2,1)S(1)} %collective-permute-done.18, bf16[768,384]{1,0:T(8,128)(2,1)S(1)} %collective-permute-done.17, bf16[768,384]{1,0:T(8,128)(2,1)} %get-tuple-element.55, bf16[768,384]{1,0:T(8,128)(2,1)S(1)} %copy-done.10, ...), kind=kLoop, calls=%fused_computation.1 | loop fusion | flops 3244032 | bytes 3540480 | tf_op jit(solution)/shard_map/convert_element_type | solution.py:602
  (84 shorter events, 23.8 us)
Async XLA Ops:
  2.5 16.8 %collective-permute-start.1 = (bf16[784,384]{1,0:T(8,128)(2,1)S(1)}, bf16[784,384]{1,0:T(8,128)(2,1)S(1)}, u32[]{:S(2)}, u32[]{:S(2)}) collective-permute-start(bf16[784,384]{1,0:T(8,128)(2,1)S(1)} %pad_maximum_fusion.1.refs_0_), channel_id=1, source_target_pairs={{0,1},{1,2},{2,3},{3,0},{4,5},{5,6},{6,7},{7,4},{8,9},{9,10},{10,1... | collective-permute-start | bytes 1806344 | tf_op jit(solution)/shard_map/ppermute | solution.py:41
  4.2 15.1 %collective-permute-start.2 = (bf16[784,384]{1,0:T(8,128)(2,1)S(1)}, bf16[784,384]{1,0:T(8,128)(2,1)S(1)}, u32[]{:S(2)}, u32[]{:S(2)}) collective-permute-start(bf16[784,384]{1,0:T(8,128)(2,1)S(1)} %pad_maximum_fusion.1.refs_0_), channel_id=1, source_target_pairs={{0,3},{1,0},{2,1},{3,2},{4,7},{5,4},{6,5},{7,6},{8,11},{9,8},{10,9... | collective-permute-start | bytes 1806344 | tf_op jit(solution)/shard_map/ppermute | solution.py:41
  5.8 17.1 %collective-permute-start = (bf16[784,384]{1,0:T(8,128)(2,1)S(1)}, bf16[784,384]{1,0:T(8,128)(2,1)S(1)}, u32[]{:S(2)}, u32[]{:S(2)}) collective-permute-start(bf16[784,384]{1,0:T(8,128)(2,1)S(1)} %pad_maximum_fusion.1.refs_0_), channel_id=1, source_target_pairs={{0,4},{1,5},{2,6},{3,7},{4,0},{5,1},{6,2},{7,3},{8,12},{9,13},{10,... | collective-permute-start | bytes 1806344 | tf_op jit(solution)/shard_map/ppermute | solution.py:41
  9.8 30.2 %collective-permute-start.6 = (bf16[2,768,384]{2,1,0:T(8,128)(2,1)}, bf16[2,768,384]{2,1,0:T(8,128)(2,1)}, u32[]{:S(2)}, u32[]{:S(2)}) collective-permute-start(bf16[2,768,384]{2,1,0:T(8,128)(2,1)} %refs_3_.1), channel_id=1, source_target_pairs={{0,16},{8,24},{16,32},{24,40},{32,48},{40,56},{48,0},{56,8},{64,80... | collective-permute-start | bytes 3538952 | tf_op jit(solution)/shard_map/ppermute | solution.py:37
  22.9 14.3 %collective-permute-start.3 = (bf16[784,384]{1,0:T(8,128)(2,1)S(1)}, bf16[784,384]{1,0:T(8,128)(2,1)S(1)}, u32[]{:S(2)}, u32[]{:S(2)}) collective-permute-start(bf16[784,384]{1,0:T(8,128)(2,1)S(1)} %collective-permute-done.refs_1_), channel_id=1, source_target_pairs={{0,3},{1,0},{2,1},{3,2},{4,7},{5,4},{6,5},{7,6},{8,11},{9,8},{10,9... | collective-permute-start | bytes 1806344 | tf_op jit(solution)/shard_map/ppermute | solution.py:41
  24.6 19.7 %copy-start.14 = (s32[8]{0:T(128)S(1)}, s32[8]{0:T(128)}, u32[]{:S(2)}) copy-start(s32[8]{0:T(128)} %constant.73.clone) | copy-start | bytes 100
  24.6 19.7 %copy-start.15 = (s32[8]{0:T(128)S(1)}, s32[8]{0:T(128)}, u32[]{:S(2)}) copy-start(s32[8]{0:T(128)} %constant.74.clone) | copy-start | bytes 100
  25.8 29.2 %collective-permute-start.5 = (bf16[2,784,384]{2,1,0:T(8,128)(2,1)}, bf16[2,784,384]{2,1,0:T(8,128)(2,1)S(1)}, u32[]{:S(2)}, u32[]{:S(2)}) collective-permute-start(bf16[2,784,384]{2,1,0:T(8,128)(2,1)} %pad_maximum_fusion), channel_id=1, source_target_pairs={{0,1},{1,2},{2,3},{3,0},{4,5},{5,6},{6,7},{7,4},{8,9},{9,10},{10,1... | collective-permute-start | bytes 3612680 | tf_op jit(solution)/shard_map/ppermute | solution.py:41
  37.2 17.7 %copy-start.8 = (bf16[784,384]{1,0:T(8,128)(2,1)}, bf16[784,384]{1,0:T(8,128)(2,1)S(1)}, u32[]{:S(2)}) copy-start(bf16[784,384]{1,0:T(8,128)(2,1)S(1)} %collective-permute-done.3.refs_0_.refs_4_) | copy-start | bytes 1806340
  37.2 17.7 %collective-permute-start.4 = (bf16[784,384]{1,0:T(8,128)(2,1)S(1)}, bf16[784,384]{1,0:T(8,128)(2,1)S(1)}, u32[]{:S(2)}, u32[]{:S(2)}) collective-permute-start(bf16[784,384]{1,0:T(8,128)(2,1)S(1)} %collective-permute-done.3.refs_0_.refs_4_), channel_id=1, source_target_pairs={{0,3},{1,0},{2,1},{3,2},{4,7},{5,4},{6,5},{7,6},{8,11},{9,8},{10,9... | collective-permute-start | bytes 1806344 | tf_op jit(solution)/shard_map/ppermute | solution.py:41
  39.9 35.7 %collective-permute-start.8 = (bf16[2,768,384]{2,1,0:T(8,128)(2,1)}, bf16[2,768,384]{2,1,0:T(8,128)(2,1)}, u32[]{:S(2)}, u32[]{:S(2)}) collective-permute-start(bf16[2,768,384]{2,1,0:T(8,128)(2,1)} %collective-permute-done.6.refs_4_), channel_id=1, source_target_pairs={{0,16},{8,24},{16,32},{24,40},{32,48},{40,56},{48,0},{56,8},{64,80... | collective-permute-start | bytes 3538952 | tf_op jit(solution)/shard_map/ppermute | solution.py:37
  41.4 36.2 %collective-permute-start.9 = (bf16[2,768,384]{2,1,0:T(8,128)(2,1)}, bf16[2,768,384]{2,1,0:T(8,128)(2,1)}, u32[]{:S(2)}, u32[]{:S(2)}) collective-permute-start(bf16[2,768,384]{2,1,0:T(8,128)(2,1)} %refs_3_.1), channel_id=1, source_target_pairs={{0,64},{8,72},{16,80},{24,88},{32,96},{40,104},{48,112},{56,120},{... | collective-permute-start | bytes 3538952 | tf_op jit(solution)/shard_map/ppermute | solution.py:37
  42.4 40.2 %collective-permute-start.10 = (bf16[2,768,384]{2,1,0:T(8,128)(2,1)}, bf16[2,768,384]{2,1,0:T(8,128)(2,1)}, u32[]{:S(2)}, u32[]{:S(2)}) collective-permute-start(bf16[2,768,384]{2,1,0:T(8,128)(2,1)} %refs_3_.1), channel_id=1, source_target_pairs={{0,48},{8,56},{16,0},{24,8},{32,16},{40,24},{48,32},{56,40},{64,11... | collective-permute-start | bytes 3538952 | tf_op jit(solution)/shard_map/ppermute | solution.py:37
  56.2 12.5 %slice-start.1 = ((s8[7077888]{0:T(1024)(128)(4,1)}), s8[2883584]{0:T(1024)(128)(4,1)S(1)}, s32[]{:S(2)}) async-start(s8[7077888]{0:T(1024)(128)(4,1)} %bitcast.14), calls=%async_computation.5 | async-start | bytes 5767168
  56.2 12.5 %copy-start = (f32[3,3072]{1,0:T(4,128)S(1)}, f32[3,3072]{1,0:T(4,128)}, u32[]{:S(2)}) copy-start(f32[3,3072]{1,0:T(4,128)} %param.18) | copy-start | bytes 110596
  56.2 12.5 %copy-start.1 = (s32[8]{0:T(128)S(1)}, s32[8]{0:T(128)}, u32[]{:S(2)}) copy-start(s32[8]{0:T(128)} %fusion.idx_ref) | copy-start | bytes 100
  56.2 12.5 %copy-start.2 = (f32[2,128]{1,0:T(2,128)S(1)}, f32[2,128]{1,0:T(2,128)}, u32[]{:S(2)}) copy-start(f32[2,128]{1,0:T(2,128)} %refs_9_.1) | copy-start | bytes 3076
  67.9 16.5 %collective-permute-start.7 = (bf16[768,384]{1,0:T(8,128)(2,1)}, bf16[768,384]{1,0:T(8,128)(2,1)S(1)}, u32[]{:S(2)}, u32[]{:S(2)}) collective-permute-start(bf16[768,384]{1,0:T(8,128)(2,1)} %get-tuple-element.35.refs_0_.q_ref), channel_id=1, source_target_pairs={{0,8},{8,0},{16,24},{24,16},{32,40},{40,32},{48,56},{56,48},{64,72... | collective-permute-start | bytes 1769480 | tf_op jit(solution)/shard_map/ppermute | solution.py:37
  71.7 40.5 %all-to-all-start = ((bf16[16,16,1152]{2,1,0:T(8,128)(2,1)}), bf16[16,16,1152]{2,1,0:T(8,128)(2,1)S(1)}, u32[]{:S(2)}, u32[]{:S(2)}) async-start(bf16[16,16,1152]{2,1,0:T(8,128)(2,1)} %broadcast_in_dim.4), calls=%async_computation | async-start | bytes 1179648 | tf_op jit(solution)/shard_map/all_to_all | solution.py:575
  75.6 40.4 %collective-permute-start.13 = (bf16[2,768,384]{2,1,0:T(8,128)(2,1)}, bf16[2,768,384]{2,1,0:T(8,128)(2,1)}, u32[]{:S(2)}, u32[]{:S(2)}) collective-permute-start(bf16[2,768,384]{2,1,0:T(8,128)(2,1)} %collective-permute-done.8.refs_2_), channel_id=1, source_target_pairs={{0,64},{8,72},{16,80},{24,88},{32,96},{40,104},{48,112},{56,120},{... | collective-permute-start | bytes 3538952 | tf_op jit(solution)/shard_map/ppermute | solution.py:37
  77.6 60.0 %collective-permute-start.15 = (bf16[384,1536]{1,0:T(8,128)(2,1)S(1)}, bf16[384,1536]{1,0:T(8,128)(2,1)}, u32[]{:S(2)}, u32[]{:S(2)}) collective-permute-start(bf16[384,1536]{1,0:T(8,128)(2,1)S(1)} %copy-done.11), channel_id=1, source_target_pairs={{0,4},{1,5},{2,6},{3,7},{4,0},{5,1},{6,2},{7,3},{8,12},{9,13},{10,... | collective-permute-start | bytes 3538952 | tf_op jit(solution)/shard_map/ppermute | solution.py:41
  81.2 34.9 %collective-permute-start.11 = (bf16[2,768,384]{2,1,0:T(8,128)(2,1)}, bf16[2,768,384]{2,1,0:T(8,128)(2,1)}, u32[]{:S(2)}, u32[]{:S(2)}) collective-permute-start(bf16[2,768,384]{2,1,0:T(8,128)(2,1)} %collective-permute-done.9.refs_3_), channel_id=1, source_target_pairs={{0,16},{8,24},{16,32},{24,40},{32,48},{40,56},{48,0},{56,8},{64,80... | collective-permute-start | bytes 3538952 | tf_op jit(solution)/shard_map/ppermute | solution.py:37
  82.7 33.4 %collective-permute-start.12 = (bf16[2,768,384]{2,1,0:T(8,128)(2,1)}, bf16[2,768,384]{2,1,0:T(8,128)(2,1)}, u32[]{:S(2)}, u32[]{:S(2)}) collective-permute-start(bf16[2,768,384]{2,1,0:T(8,128)(2,1)} %collective-permute-done.9.refs_3_), channel_id=1, source_target_pairs={{0,48},{8,56},{16,0},{24,8},{32,16},{40,24},{48,32},{56,40},{64,11... | collective-permute-start | bytes 3538952 | tf_op jit(solution)/shard_map/ppermute | solution.py:37
  131.4 6.2 %collective-permute-start.14 = (bf16[2,768,384]{2,1,0:T(8,128)(2,1)}, bf16[2,768,384]{2,1,0:T(8,128)(2,1)}, u32[]{:S(2)}, u32[]{:S(2)}) collective-permute-start(bf16[2,768,384]{2,1,0:T(8,128)(2,1)} %get-tuple-element.52), channel_id=1, source_target_pairs={{0,8},{8,0},{16,24},{24,16},{32,40},{40,32},{48,56},{56,48},{64,72... | collective-permute-start | bytes 3538952 | tf_op jit(solution)/shard_map/ppermute | solution.py:37
  132.3 12.8 %all-to-all-start.1 = ((bf16[16,2,16,384]{3,2,1,0:T(8,128)(2,1)}), bf16[16,2,16,384]{3,2,1,0:T(8,128)(2,1)S(1)}, u32[]{:S(2)}, u32[]{:S(2)}) async-start(bf16[16,2,16,384]{3,2,1,0:T(8,128)(2,1)} %text_attention.1), calls=%async_computation.1 | async-start | bytes 786432 | tf_op jit(solution)/shard_map/all_to_all | solution.py:584
  141.7 17.4 %collective-permute-start.16 = (bf16[768,384]{1,0:T(8,128)(2,1)}, bf16[768,384]{1,0:T(8,128)(2,1)S(1)}, u32[]{:S(2)}, u32[]{:S(2)}) collective-permute-start(bf16[768,384]{1,0:T(8,128)(2,1)} %quotient.1.mine_ref), channel_id=1, source_target_pairs={{0,4},{1,5},{2,6},{3,7},{4,0},{5,1},{6,2},{7,3},{8,12},{9,13},{10,... | collective-permute-start | bytes 1769480 | tf_op jit(solution)/shard_map/ppermute | solution.py:41
  149.1 20.4 %all-to-all-start.2 = ((bf16[8,16,384]{2,1,0:T(8,128)(2,1)}), bf16[8,16,384]{2,1,0:T(8,128)(2,1)S(1)}, u32[]{:S(2)}, u32[]{:S(2)}) async-start(bf16[8,16,384]{2,1,0:T(8,128)(2,1)} %text_quotient.1), calls=%async_computation.2 | async-start | bytes 196608 | tf_op jit(solution)/shard_map/all_to_all | solution.py:603
  166.2 28.2 %copy-start.10 = (bf16[768,384]{1,0:T(8,128)(2,1)S(1)}, bf16[768,384]{1,0:T(8,128)(2,1)}, u32[]{:S(2)}) copy-start(bf16[768,384]{1,0:T(8,128)(2,1)} %param.14) | copy-start | bytes 1769476
  166.2 27.6 %collective-permute-start.17 = (bf16[768,384]{1,0:T(8,128)(2,1)}, bf16[768,384]{1,0:T(8,128)(2,1)S(1)}, u32[]{:S(2)}, u32[]{:S(2)}) collective-permute-start(bf16[768,384]{1,0:T(8,128)(2,1)} %get-tuple-element.56), channel_id=1, source_target_pairs={{0,1},{1,2},{2,3},{3,0},{4,5},{5,6},{6,7},{7,4},{8,9},{9,10},{10,1... | collective-permute-start | bytes 1769480 | tf_op jit(solution)/shard_map/ppermute | solution.py:41
  166.3 27.5 %collective-permute-start.18 = (bf16[768,384]{1,0:T(8,128)(2,1)}, bf16[768,384]{1,0:T(8,128)(2,1)S(1)}, u32[]{:S(2)}, u32[]{:S(2)}) collective-permute-start(bf16[768,384]{1,0:T(8,128)(2,1)} %get-tuple-element.57), channel_id=1, source_target_pairs={{0,2},{1,3},{2,0},{3,1},{4,6},{5,7},{6,4},{7,5},{8,10},{9,11},{10,... | collective-permute-start | bytes 1769480 | tf_op jit(solution)/shard_map/ppermute | solution.py:41
  166.8 27.6 %collective-permute-start.19 = (bf16[768,384]{1,0:T(8,128)(2,1)}, bf16[768,384]{1,0:T(8,128)(2,1)S(1)}, u32[]{:S(2)}, u32[]{:S(2)}) collective-permute-start(bf16[768,384]{1,0:T(8,128)(2,1)} %get-tuple-element.58), channel_id=1, source_target_pairs={{0,3},{1,0},{2,1},{3,2},{4,7},{5,4},{6,5},{7,6},{8,11},{9,8},{10,9... | collective-permute-start | bytes 1769480 | tf_op jit(solution)/shard_map/ppermute | solution.py:41
  171.0 12.1 %all-to-all-start.3 = ((bf16[16,16,384]{2,1,0:T(8,128)(2,1)}), bf16[16,16,384]{2,1,0:T(8,128)(2,1)S(1)}, u32[]{:S(2)}, u32[]{:S(2)}) async-start(bf16[16,16,384]{2,1,0:T(8,128)(2,1)} %broadcast_in_dim.5), calls=%async_computation.3 | async-start | bytes 393216 | tf_op jit(solution)/shard_map/all_to_all | solution.py:606
  (12 other events, 50.7 us)
where the time goes:
time: 199 us; the launch traced here: 197 us
  Pallas kernels  82.9 us (42%)
  waiting for transfers between devices  49 us (25%)
  starting transfers between devices  46.1 us (23%)
  local copies, waits for them, and re-layouts  11.3 us (6%)
  other arithmetic  6.59 us (3%)
    pallas_call x3, Pallas kernels, attention(): pl.pallas_call(functools.partial(att_kernel, plan=plan, n_q=n_q, n_kv=len...  42.3 us
    ppermute x11, waiting for transfers between devices, send_head(): return lax.ppermute(x, 'head', head_perm(dz, dy))  40 us
    ppermute x11, starting transfers between devices, send_head(): return lax.ppermute(x, 'head', head_perm(dz, dy))  18.9 us
    pallas_call x1, Pallas kernels, late_qkv(): pl.pallas_call(functools.partial(late_kernel, first=first, tile=tile, sca...  11.7 us
    ppermute x9, starting transfers between devices, send_patch(): return lax.ppermute(x, 'patch', patch_perm(dz, dx, dc))  11.3 us
    pallas_call x1, Pallas kernels, early_qkv(): pl.pallas_call(functools.partial(early_kernel, blocks=n, rows=rows), in_s...  10.1 us
    pallas_call x1, Pallas kernels, project(): pl.pallas_call(proj_kernel, in_specs=[pl.BlockSpec(memory_space=pltpu.SME...  6.31 us
    all_to_all x1, waiting for transfers between devices, shards(): lax.all_to_all(jnp.broadcast_to(t_out[None], (n_patch,) + t_out.shape), '...  6.26 us
  transfers between devices with their start and end apart: 24, of which 9 were waited for; matrix products, arithmetic and copies ran while one was open for 4% of the time, Pallas kernels for 42%

commit v1 on v0

--- a/solution.py
+++ b/solution.py
@@ -321,9 +321,8 @@
             refs.pop(0)[...] = den
 
 
-def attention(pos, qs, kvs, plan, text=None, acc=None, packed=(), rows=None, chunk=0, width=None, name="att"):
-    width = qs[0].shape[1] if width is None else width
-    rows = qs[0].shape[0] if rows is None else rows
+def attention(pos, qs, kvs, plan, text=None, acc=None, packed=(), name="att"):
+    rows, width = qs[0].shape
     hd = 128
     heads = width // hd
     n_q = len(qs)
@@ -331,7 +330,7 @@
     if text is not None:
         args.append(text[0])
         specs.append(pl.BlockSpec(memory_space=pltpu.SMEM))
-    q_spec = pl.BlockSpec((rows, hd), lambda h, p: (chunk, h))
+    q_spec = pl.BlockSpec((rows, hd), lambda h, p: (0, h))
     out_spec = pl.BlockSpec((rows, hd), lambda h, p: (0, h))
     for q in qs:
         args.append(q)
@@ -410,13 +409,12 @@
 
 def image_quotient(len_ref, q_ref, txt_ref, num_ref, den_ref, got_ref, attn_ref):
     hd = 128
-    rows = num_ref.shape[0]
     for h in range(num_ref.shape[1] // hd):
         cols = slice(h * hd, (h + 1) * hd)
         n, d = text_keys(q_ref, txt_ref, len_ref, h)
         num = n + num_ref[:, cols] + got_ref[0, :, cols].astype(F32)
         den = d + den_ref[:, cols] + got_ref[1, :, cols].astype(F32)
-        attn_ref[0:rows, cols] = (num / den).astype(BF)
+        attn_ref[:, cols] = (num / den).astype(BF)
 
 
 def quotient(text_len, q, txt, num, den, got):
@@ -461,23 +459,28 @@
     )(text_len, sums, q, txt, proj)
 
 
-def proj_kernel(pos_ref, mine_ref, got_ref, w_ref, wz_ref, *refs):
+def proj_kernel(pos_ref, mine_ref, got_ref, w_ref, wz_ref, wc_ref, *refs):
     outs = refs[:NY]
     w_buf, sem = refs[NY:]
     width = mine_ref.shape[1]
-    zh, y = pos_ref[0], pos_ref[1]
+    zh, y, core = pos_ref[0], pos_ref[1], pos_ref[2]
+    half = width // 2
     order = (2, 1, 3, 0)
 
     def copies(d):
         block = lax.rem(y + d, NY)
-        pairs = ((w_ref, zh * NY + block), (wz_ref, block))
+        sources = (
+            (w_ref, zh * NY + block, 0, width),
+            (wz_ref, block, width + core * half, half),
+            (wc_ref, block, width + (1 - core) * half, half),
+        )
         return [
             pltpu.make_async_copy(
                 ref.at[:, pl.ds(pl.multiple_of(at * width, 128), width)],
-                w_buf.at[d, pl.ds(i * width, width)],
+                w_buf.at[d, pl.ds(row if i == 0 else pl.multiple_of(row, half), size)],
                 sem.at[d, i],
             )
-            for i, (ref, at) in enumerate(pairs)
+            for i, (ref, at, row, size) in enumerate(sources)
         ]
 
     for d in order:
@@ -490,23 +493,23 @@
         outs[d][...] = jnp.dot(both, w_buf[d], preferred_element_type=F32).astype(BF)
 
 
-def project(pos, mine, got, w, wz):
+def project(pos, mine, got, w, wz, wc):
     width = mine.shape[1]
     spec = pl.BlockSpec(memory_space=pltpu.VMEM)
     hbm = pl.BlockSpec(memory_space=pltpu.HBM)
     return pl.pallas_call(
         proj_kernel,
-        in_specs=[pl.BlockSpec(memory_space=pltpu.SMEM)] + [spec] * 2 + [hbm] * 2,
+        in_specs=[pl.BlockSpec(memory_space=pltpu.SMEM)] + [spec] * 2 + [hbm] * 3,
         out_specs=[spec] * NY,
         out_shape=[jax.ShapeDtypeStruct(mine.shape, BF)] * NY,
         scratch_shapes=[
             pltpu.VMEM((NY, 2 * width, width), BF),
-            pltpu.SemaphoreType.DMA((NY, 2)),
+            pltpu.SemaphoreType.DMA((NY, 3)),
         ],
         compiler_params=pltpu.CompilerParams(vmem_limit_bytes=VMEM),
         cost_estimate=cost(6),
         name="project",
-    )(pos, mine, got, w, wz)
+    )(pos, mine, got, w, wz, wc)
 
 
 def exchange(parts):
@@ -539,7 +542,7 @@
     txt_total = text.shape[0]
     t_rows = txt_total // n_patch
 
-    pos = jnp.stack([zh, y]).astype(jnp.int32)
+    pos = jnp.stack([zh, y, me_p % 2]).astype(jnp.int32)
 
     t_own = lax.dynamic_slice_in_dim(text, me_p * t_rows, t_rows, 0)
     rows = jnp.concatenate([image, t_own], axis=0)
@@ -547,7 +550,10 @@
     i_m = send_head(rows, dy=1)
     i_p = send_head(rows, dy=-1)
     kv_m = send_patch(stale_kv, dx=1)
-    part_z = lax.dynamic_slice_in_dim(img_proj, (1 - zh) * NY * width, NY * width, 1)
+    core = me_p % 2
+    part_z = lax.dynamic_slice(
+        img_proj, (core * (width // 2), (1 - zh) * NY * width), (width // 2, NY * width)
+    )
     near = after(i_z, i_m, i_p, part_z)
     ahead = send_head(jnp.stack([i_m, near]), dy=1)
     iz_p = send_head(near, dy=-1)
@@ -567,6 +573,7 @@
     kvz_p = send_patch(kv_z, dx=-1)
     kvz_2 = send_patch(kv_2, dz=1)
     proj_z = send_head(after(part_z, kv_z), dz=1)
+    proj_c = send_patch(proj_z, dc=1)
     q, kv = late_qkv(idx, [iz_p, iz_2, ahead], w_i, acc, stat, mod_i, img_gain)
     x_list = [rows, near, i_m, i_p, iz_p, iz_2, ahead]
     q_c = send_patch(q, dc=1)
@@ -577,9 +584,12 @@
     ).reshape(txt_total, 3 * width)
 
     both = attention(
-        after(pos, t_pack), [q, q_c], [kv, stale_kv, kv_m, kv_p], [[0, 2, 3], [1, 2, 3]], name="att_near"
+        after(pos, t_pack),
+        [q, q_c],
+        [kv, stale_kv, kv_m, kv_p, kv_2, kv_z],
+        [[0, 2, 3, 4, 5], [1, 2, 3, 4, 5]],
+        name="att_near",
     )
-    both = attention(pos, [q, q_c], [kv_2, kv_z], [[0, 1]] * 2, acc=both, name="att_mid")
     t_sums = text_attention(after(txt, both[0]), kv, n_patch)
     t_got = lax.all_to_all(t_sums, "patch", 0, 0)
     num, den, part_c = attention(
@@ -592,11 +602,10 @@
         name="att_last",
     )
     got_c = send_patch(part_c, dc=1)
-    attn = quotient(text_len, q, txt, num, den, after(got_c, proj_z))
+    attn = quotient(text_len, q, txt, num, den, after(got_c, proj_c))
     from_z = send_head(attn, dz=1)
     t_proj = text_quotient(text_len, after(t_got, attn), t_q, txt, txt_proj, n_head)
-    outs = project(pos, attn, from_z, img_proj, proj_z)
-    img_sum = exchange(outs)
+    img_sum = exchange(project(pos, attn, from_z, img_proj, proj_z, proj_c))
     column = me_h * width
     img_gate = lax.dynamic_slice_in_dim(img_mod[2], column, width)
     img_out = (image.astype(F32) + img_gate * img_sum).astype(BF)

time: 199 us -> 196 us (0.985)
  starting transfers between devices: 46.1 us -> 50.9 us
  Pallas kernels: 82.9 us -> 78.9 us
    pallas_call x3 -> x2, Pallas kernels: 42.3 us -> 38.2 us  [attention(): pl.pallas_call(functools.partial(att_kernel, plan=plan, n_q=n_q, n_kv=len...]
    ppermute x11, starting transfers between devices: 18.9 us -> 22.4 us  [send_head(): return lax.ppermute(x, 'head', head_perm(dz, dy))]
    unnamed x41 -> x39, local copies, waits for them, and re-layouts: 5.17 us -> 3.96 us
    ppermute x9 -> x10, starting transfers between devices: 11.3 us -> 11.8 us  [send_patch(): return lax.ppermute(x, 'patch', patch_perm(dz, dx, dc))]
  transfers between devices with their start and end apart: 24 -> 25, of which waited for: 9 -> 8; matrix products, arithmetic and copies ran while one was open for 4% -> 4% of each run, Pallas kernels for 42% -> 41%
where the time goes in v1:
time: 196 us; the launch traced here: 195 us
  Pallas kernels  78.9 us (40%)
  starting transfers between devices  50.9 us (26%)
  waiting for transfers between devices  47.2 us (24%)
  local copies, waits for them, and re-layouts  9.67 us (5%)
  other arithmetic  6.6 us (3%)
    ppermute x11, waiting for transfers between devices, send_head(): return lax.ppermute(x, 'head', head_perm(dz, dy))  40.1 us
    pallas_call x2, Pallas kernels, attention(): pl.pallas_call(functools.partial(att_kernel, plan=plan, n_q=n_q, n_kv=len...  38.2 us
    ppermute x11, starting transfers between devices, send_head(): return lax.ppermute(x, 'head', head_perm(dz, dy))  22.4 us
    ppermute x10, starting transfers between devices, send_patch(): return lax.ppermute(x, 'patch', patch_perm(dz, dx, dc))  11.8 us
    pallas_call x1, Pallas kernels, late_qkv(): pl.pallas_call(functools.partial(late_kernel, first=first, tile=tile, sca...  11.5 us
    pallas_call x1, Pallas kernels, early_qkv(): pl.pallas_call(functools.partial(early_kernel, blocks=n, rows=rows), in_s...  10.1 us
    pallas_call x1, Pallas kernels, project(): pl.pallas_call(proj_kernel, in_specs=[pl.BlockSpec(memory_space=pltpu.SME...  6.38 us
    all_to_all x1, waiting for transfers between devices, shards(): lax.all_to_all(jnp.broadcast_to(t_out[None], (n_patch,) + t_out.shape), '...  6.26 us
  transfers between devices with their start and end apart: 25, of which 8 were waited for; matrix products, arithmetic and copies ran while one was open for 4% of the time, Pallas kernels for 41%

profile of v1, /device:TPU:0, one launch (start us, length us, event | category | flops | bytes accessed | tf_op | source)
XLA Modules:
  0.0 194.8 jit_solution(5543551652424207408)
XLA Ops:
  2.5 1.7 collective-permute-start.1
  4.2 1.6 collective-permute-start.2
  5.8 4.0 %collective-permute-start = (bf16[784,384]{1,0:T(8,128)(2,1)S(1)}, bf16[784,384]{1,0:T(8,128)(2,1)S(1)}, u32[]{:S(2)}, u32[]{:S(2)}) collective-permute-start(bf16[784,384]{1,0:T(8,128)(2,1)S(1)} %pad_maximum_fusion.1.refs_0_), channel_id=1, source_target_pairs={{0,4},{1,5},{2,6},{3,7},{4,0},{5,1},{6,2},{7,3},{8,12},{9,13},{10,... | collective-permute-start | bytes 1806344 | tf_op jit(solution)/shard_map/ppermute | solution.py:41
  11.2 2.0 %dynamic_slice.14 = bf16[192,1536]{1,0:T(8,128)(2,1)} dynamic-slice(bf16[384,3072]{1,0:T(8,128)(2,1)} %w_ref.1, s32[]{:T(128)S(6)} %select_n.47, s32[]{:T(128)S(6)} %select_n.48), dynamic_slice_sizes={192,1536} | dynamic-slice | bytes 1179652 | tf_op jit(solution)/shard_map/dynamic_slice | solution.py:554
  13.2 6.0 %collective-permute-done.1.refs_2_ = bf16[784,384]{1,0:T(8,128)(2,1)S(1)} collective-permute-done((bf16[784,384]{1,0:T(8,128)(2,1)S(1)}, bf16[784,384]{1,0:T(8,128)(2,1)S(1)}, u32[]{:S(2)}, u32[]{:S(2)}) %collective-permute-start.1) | collective-permute-done | bytes 602144 | tf_op jit(solution)/shard_map/ppermute | solution.py:41
  19.3 3.7 %collective-permute-done.refs_1_ = bf16[784,384]{1,0:T(8,128)(2,1)S(1)} collective-permute-done((bf16[784,384]{1,0:T(8,128)(2,1)S(1)}, bf16[784,384]{1,0:T(8,128)(2,1)S(1)}, u32[]{:S(2)}, u32[]{:S(2)}) %collective-permute-start) | collective-permute-done | bytes 602144 | tf_op jit(solution)/shard_map/ppermute | solution.py:41
  22.9 1.7 collective-permute-start.3
  26.2 11.1 %collective-permute-done.3.refs_0_.refs_4_ = bf16[784,384]{1,0:T(8,128)(2,1)} collective-permute-done((bf16[784,384]{1,0:T(8,128)(2,1)S(1)}, bf16[784,384]{1,0:T(8,128)(2,1)}, u32[]{:S(2)}, u32[]{:S(2)}) %collective-permute-start.3) | collective-permute-done | bytes 602144 | tf_op jit(solution)/shard_map/ppermute | solution.py:41
  37.3 2.7 %collective-permute-start.4 = (bf16[784,384]{1,0:T(8,128)(2,1)}, bf16[784,384]{1,0:T(8,128)(2,1)S(1)}, u32[]{:S(2)}, u32[]{:S(2)}) collective-permute-start(bf16[784,384]{1,0:T(8,128)(2,1)} %collective-permute-done.3.refs_0_.refs_4_), channel_id=1, source_target_pairs={{0,3},{1,0},{2,1},{3,2},{4,7},{5,4},{6,5},{7,6},{8,11},{9,8},{10,9... | collective-permute-start | bytes 1806344 | tf_op jit(solution)/shard_map/ppermute | solution.py:41
  42.5 1.9 collective-permute-start.8
  45.0 10.1 %early_qkv.1 = (f32[784,1152]{1,0:T(8,128)}, f32[2,768,128]{2,1,0:T(8,128)}) custom-call(s32[8]{0:T(128)} %fusion.idx_ref, bf16[784,384]{1,0:T(8,128)(2,1)} %copy-done.3, bf16[784,384]{1,0:T(8,128)(2,1)} %copy-done.5, bf16[784,384]{1,0:T(8,128)(2,1)} %copy-done.4, bf16[784,384]{1,0:T(8,128)(2,1)} %copy-done.6, bf16[3,3072,384]{2,1,0:T(8,128)(2,1)} %bitcast.19, ...), custom_call_target="tpu_custom_call" | custom-call | flops 1 | bytes 1 | tf_op jit(solution)/shard_map/early_qkv/pallas_call | solution.py:195
  55.9 11.5 %late_qkv.1 = (bf16[768,384]{1,0:T(8,128)(2,1)}, bf16[2,768,384]{2,1,0:T(8,128)(2,1)}) custom-call(s32[8]{0:T(128)} %fusion.idx_ref, bf16[784,384]{1,0:T(8,128)(2,1)} %collective-permute-done.3.refs_0_.refs_4_, bf16[784,384]{1,0:T(8,128)(2,1)} %copy-done.7, bf16[2,784,384]{2,1,0:T(8,128)(2,1)} %collective-permute-done.5.refs_2_.refs_6_, ...), custom_call_target="tpu_custom_call" | custom-call | flops 1 | bytes 1 | tf_op jit(solution)/shard_map/late_qkv/pallas_call | solution.py:223
  68.3 2.1 %text_qkv.1 = bf16[16,1152]{1,0:T(8,128)(2,1)S(1)} custom-call(s32[8]{0:T(128)S(1)} %copy-done.1, bf16[784,384]{1,0:T(8,128)(2,1)} %copy-done.3, bf16[784,384]{1,0:T(8,128)(2,1)} %copy-done.5, bf16[784,384]{1,0:T(8,128)(2,1)} %copy-done.4, bf16[784,384]{1,0:T(8,128)(2,1)} %copy-done.6, bf16[784,384]{1,0:T(8,128)(2,1)} %collective-permute-done.3.refs_0_.refs_4_, ...), custom_call_target="tpu_custom_call" | custom-call | flops 2300000000 | bytes 1 | tf_op jit(solution)/shard_map/text_qkv/pallas_call | solution.py:270
  71.2 4.0 %all-to-all-start = ((bf16[16,16,1152]{2,1,0:T(8,128)(2,1)}), bf16[16,16,1152]{2,1,0:T(8,128)(2,1)S(1)}, u32[]{:S(2)}, u32[]{:S(2)}) async-start(bf16[16,16,1152]{2,1,0:T(8,128)(2,1)} %broadcast_in_dim.4), calls=%async_computation | async-start | bytes 1179648 | tf_op jit(solution)/shard_map/all_to_all | solution.py:582
  75.3 2.0 %collective-permute-start.13 = (bf16[2,768,384]{2,1,0:T(8,128)(2,1)}, bf16[2,768,384]{2,1,0:T(8,128)(2,1)}, u32[]{:S(2)}, u32[]{:S(2)}) collective-permute-start(bf16[2,768,384]{2,1,0:T(8,128)(2,1)} %collective-permute-done.9.refs_6_), channel_id=1, source_target_pairs={{0,64},{8,72},{16,80},{24,88},{32,96},{40,104},{48,112},{56,120},{... | collective-permute-start | bytes 3538952 | tf_op jit(solution)/shard_map/ppermute | solution.py:37
  77.3 3.6 %collective-permute-start.15 = (bf16[192,1536]{1,0:T(8,128)(2,1)S(1)}, bf16[192,1536]{1,0:T(8,128)(2,1)S(1)}, u32[]{:S(2)}, u32[]{:S(2)}) collective-permute-start(bf16[192,1536]{1,0:T(8,128)(2,1)S(1)} %copy-done.10), channel_id=1, source_target_pairs={{0,4},{1,5},{2,6},{3,7},{4,0},{5,1},{6,2},{7,3},{8,12},{9,13},{10,... | collective-permute-start | bytes 1769480 | tf_op jit(solution)/shard_map/ppermute | solution.py:41
  82.3 1.8 collective-permute-start.12
  84.9 22.8 %att_near.1 = (f32[768,384]{1,0:T(8,128)}, f32[768,384]{1,0:T(8,128)}, f32[768,384]{1,0:T(8,128)}, f32[768,384]{1,0:T(8,128)}) custom-call(s32[3]{0:T(128)} %pad_add_fusion.pos_ref, bf16[768,384]{1,0:T(8,128)(2,1)} %get-tuple-element.31.refs_0_.q_ref, bf16[768,384]{1,0:T(8,128)(2,1)} %copy-done.15, bf16[2,768,384]{2,1,0:T(8,128)(2,1)} %get-tuple-element.34.refs_2_.kv_ref, ...), custom_call_target="tpu_custom_call" | custom-call | flops 31708938240 | bytes 1 | tf_op jit(solution)/shard_map/att_near/pallas_call | solution.py:360
  108.5 3.0 %text_attention.1 = bf16[16,2,16,384]{3,2,1,0:T(8,128)(2,1)} custom-call(bf16[256,1152]{1,0:T(8,128)(2,1)} %bitcast.24, bf16[2,768,384]{2,1,0:T(8,128)(2,1)} %get-tuple-element.34.refs_2_.kv_ref), custom_call_target="tpu_custom_call" | custom-call | flops 3449999872 | bytes 1 | tf_op jit(solution)/shard_map/text_attention/pallas_call | solution.py:389
  111.6 15.4 %att_last.1 = (f32[768,384]{1,0:T(8,128)}, f32[768,384]{1,0:T(8,128)}, bf16[2,768,384]{2,1,0:T(8,128)(2,1)}) custom-call(s32[3]{0:T(128)} %pad_add_fusion.pos_ref, bf16[768,384]{1,0:T(8,128)(2,1)} %get-tuple-element.31.refs_0_.q_ref, bf16[768,384]{1,0:T(8,128)(2,1)} %copy-done.15, bf16[2,768,384]{2,1,0:T(8,128)(2,1)} %collective-permute-done.11.refs_2_, ...), custom_call_target="tpu_custom_call" | custom-call | flops 19025362944 | bytes 1 | tf_op jit(solution)/shard_map/att_last/pallas_call | solution.py:360
  128.3 3.6 %all-to-all-start.1 = ((bf16[16,2,16,384]{3,2,1,0:T(8,128)(2,1)}), bf16[16,2,16,384]{3,2,1,0:T(8,128)(2,1)S(1)}, u32[]{:S(2)}, u32[]{:S(2)}) async-start(bf16[16,2,16,384]{3,2,1,0:T(8,128)(2,1)} %text_attention.1), calls=%async_computation.1 | async-start | bytes 786432 | tf_op jit(solution)/shard_map/all_to_all | solution.py:594
  131.9 4.3 %quotient.1.mine_ref = bf16[768,384]{1,0:T(8,128)(2,1)} custom-call(s32[1]{0:T(128)S(6)} %copy.17.len_ref, bf16[768,384]{1,0:T(8,128)(2,1)} %get-tuple-element.31.refs_0_.q_ref, bf16[256,1152]{1,0:T(8,128)(2,1)} %bitcast.25, f32[768,384]{1,0:T(8,128)} %get-tuple-element.42.num_ref, f32[768,384]{1,0:T(8,128)} %get-tuple-element.43.den_ref, ...), custom_call_target="tpu_custom_call" | custom-call | flops 4600000000 | bytes 1 | tf_op jit(solution)/shard_map/quotient/pallas_call | solution.py:422
  136.2 3.5 %collective-permute-start.17 = (bf16[768,384]{1,0:T(8,128)(2,1)}, bf16[768,384]{1,0:T(8,128)(2,1)}, u32[]{:S(2)}, u32[]{:S(2)}) collective-permute-start(bf16[768,384]{1,0:T(8,128)(2,1)} %quotient.1.mine_ref), channel_id=1, source_target_pairs={{0,4},{1,5},{2,6},{3,7},{4,0},{5,1},{6,2},{7,3},{8,12},{9,13},{10,... | collective-permute-start | bytes 1769480 | tf_op jit(solution)/shard_map/ppermute | solution.py:41
  141.8 3.4 %text_quotient.1 = bf16[8,16,384]{2,1,0:T(8,128)(2,1)} custom-call(s32[1]{0:T(128)S(6)} %copy.17.len_ref, bf16[16,2,16,384]{3,2,1,0:T(8,128)(2,1)} %copy-done.11, bf16[16,384]{1,0:T(8,128)(2,1)} %slice.12.q_ref, bf16[256,1152]{1,0:T(8,128)(2,1)} %bitcast.26, bf16[384,3072]{1,0:T(8,128)(2,1)} %proj_ref.1), custom_call_target="tpu_custom_call" | custom-call | flops 4600000000 | bytes 1 | tf_op jit(solution)/shard_map/text_quotient/pallas_call | solution.py:451
  145.1 4.8 %all-to-all-start.2 = ((bf16[8,16,384]{2,1,0:T(8,128)(2,1)}), bf16[8,16,384]{2,1,0:T(8,128)(2,1)S(1)}, u32[]{:S(2)}, u32[]{:S(2)}) async-start(bf16[8,16,384]{2,1,0:T(8,128)(2,1)} %text_quotient.1), calls=%async_computation.2 | async-start | bytes 196608 | tf_op jit(solution)/shard_map/all_to_all | solution.py:612
  149.9 5.5 %collective-permute-done.17.got_ref = bf16[768,384]{1,0:T(8,128)(2,1)} collective-permute-done((bf16[768,384]{1,0:T(8,128)(2,1)}, bf16[768,384]{1,0:T(8,128)(2,1)}, u32[]{:S(2)}, u32[]{:S(2)}) %collective-permute-start.17) | collective-permute-done | bytes 589856 | tf_op jit(solution)/shard_map/ppermute | solution.py:41
  155.4 6.4 %project.1 = (bf16[768,384]{1,0:T(8,128)(2,1)}, bf16[768,384]{1,0:T(8,128)(2,1)}, bf16[768,384]{1,0:T(8,128)(2,1)}, bf16[768,384]{1,0:T(8,128)(2,1)}) custom-call(s32[3]{0:T(128)} %pad_add_fusion.pos_ref, bf16[768,384]{1,0:T(8,128)(2,1)} %quotient.1.mine_ref, bf16[768,384]{1,0:T(8,128)(2,1)} %collective-permute-done.17.got_ref, bf16[384,3072]{1,0:T(8,128)(2,1)} %w_ref.1, ...), custom_call_target="tpu_custom_call" | custom-call | flops 6899999744 | bytes 1 | tf_op jit(solution)/shard_map/project/pallas_call | solution.py:500
  163.4 1.7 collective-permute-start.20
  166.6 4.3 %all-to-all-start.3 = ((bf16[16,16,384]{2,1,0:T(8,128)(2,1)}), bf16[16,16,384]{2,1,0:T(8,128)(2,1)S(1)}, u32[]{:S(2)}, u32[]{:S(2)}) async-start(bf16[16,16,384]{2,1,0:T(8,128)(2,1)} %broadcast_in_dim.5), calls=%async_computation.3 | async-start | bytes 393216 | tf_op jit(solution)/shard_map/all_to_all | solution.py:615
  171.8 6.3 %all-to-all-done.3 = bf16[16,16,384]{2,1,0:T(8,128)(2,1)S(1)} async-done(((bf16[16,16,384]{2,1,0:T(8,128)(2,1)}), bf16[16,16,384]{2,1,0:T(8,128)(2,1)S(1)}, u32[]{:S(2)}, u32[]{:S(2)}) %all-to-all-start.3) | async-done | bytes 196640 | tf_op jit(solution)/shard_map/all_to_all | solution.py:615
  178.0 13.2 %collective-permute-done.18 = bf16[768,384]{1,0:T(8,128)(2,1)S(1)} collective-permute-done((bf16[768,384]{1,0:T(8,128)(2,1)}, bf16[768,384]{1,0:T(8,128)(2,1)S(1)}, u32[]{:S(2)}, u32[]{:S(2)}) %collective-permute-start.18) | collective-permute-done | bytes 589856 | tf_op jit(solution)/shard_map/ppermute | solution.py:41
  191.8 2.3 %add_convert_fusion = bf16[768,384]{1,0:T(8,128)(2,1)} fusion(bf16[768,384]{1,0:T(8,128)(2,1)S(1)} %collective-permute-done.20, bf16[768,384]{1,0:T(8,128)(2,1)S(1)} %collective-permute-done.19, bf16[768,384]{1,0:T(8,128)(2,1)S(1)} %collective-permute-done.18, bf16[768,384]{1,0:T(8,128)(2,1)} %get-tuple-element.47, bf16[768,384]{1,0:T(8,128)(2,1)S(1)} %copy-done.8, ...), kind=kLoop, calls=%fused_computation.1 | loop fusion | flops 3244032 | bytes 3540480 | tf_op jit(solution)/shard_map/convert_element_type | solution.py:611
  (83 shorter events, 21.7 us)
Async XLA Ops:
  2.5 23.3 %copy-start.3 = (bf16[784,384]{1,0:T(8,128)(2,1)}, bf16[784,384]{1,0:T(8,128)(2,1)S(1)}, u32[]{:S(2)}) copy-start(bf16[784,384]{1,0:T(8,128)(2,1)S(1)} %pad_maximum_fusion.1.refs_0_) | copy-start | bytes 1806340
  2.5 16.8 %collective-permute-start.1 = (bf16[784,384]{1,0:T(8,128)(2,1)S(1)}, bf16[784,384]{1,0:T(8,128)(2,1)S(1)}, u32[]{:S(2)}, u32[]{:S(2)}) collective-permute-start(bf16[784,384]{1,0:T(8,128)(2,1)S(1)} %pad_maximum_fusion.1.refs_0_), channel_id=1, source_target_pairs={{0,1},{1,2},{2,3},{3,0},{4,5},{5,6},{6,7},{7,4},{8,9},{9,10},{10,1... | collective-permute-start | bytes 1806344 | tf_op jit(solution)/shard_map/ppermute | solution.py:41
  4.2 15.1 %collective-permute-start.2 = (bf16[784,384]{1,0:T(8,128)(2,1)S(1)}, bf16[784,384]{1,0:T(8,128)(2,1)S(1)}, u32[]{:S(2)}, u32[]{:S(2)}) collective-permute-start(bf16[784,384]{1,0:T(8,128)(2,1)S(1)} %pad_maximum_fusion.1.refs_0_), channel_id=1, source_target_pairs={{0,3},{1,0},{2,1},{3,2},{4,7},{5,4},{6,5},{7,6},{8,11},{9,8},{10,9... | collective-permute-start | bytes 1806344 | tf_op jit(solution)/shard_map/ppermute | solution.py:41
  5.8 17.1 %collective-permute-start = (bf16[784,384]{1,0:T(8,128)(2,1)S(1)}, bf16[784,384]{1,0:T(8,128)(2,1)S(1)}, u32[]{:S(2)}, u32[]{:S(2)}) collective-permute-start(bf16[784,384]{1,0:T(8,128)(2,1)S(1)} %pad_maximum_fusion.1.refs_0_), channel_id=1, source_target_pairs={{0,4},{1,5},{2,6},{3,7},{4,0},{5,1},{6,2},{7,3},{8,12},{9,13},{10,... | collective-permute-start | bytes 1806344 | tf_op jit(solution)/shard_map/ppermute | solution.py:41
  9.8 30.3 %collective-permute-start.6 = (bf16[2,768,384]{2,1,0:T(8,128)(2,1)}, bf16[2,768,384]{2,1,0:T(8,128)(2,1)}, u32[]{:S(2)}, u32[]{:S(2)}) collective-permute-start(bf16[2,768,384]{2,1,0:T(8,128)(2,1)} %refs_3_.1), channel_id=1, source_target_pairs={{0,16},{8,24},{16,32},{24,40},{32,48},{40,56},{48,0},{56,8},{64,80... | collective-permute-start | bytes 3538952 | tf_op jit(solution)/shard_map/ppermute | solution.py:37
  22.9 14.4 %collective-permute-start.3 = (bf16[784,384]{1,0:T(8,128)(2,1)S(1)}, bf16[784,384]{1,0:T(8,128)(2,1)}, u32[]{:S(2)}, u32[]{:S(2)}) collective-permute-start(bf16[784,384]{1,0:T(8,128)(2,1)S(1)} %collective-permute-done.refs_1_), channel_id=1, source_target_pairs={{0,3},{1,0},{2,1},{3,2},{4,7},{5,4},{6,5},{7,6},{8,11},{9,8},{10,9... | collective-permute-start | bytes 1806344 | tf_op jit(solution)/shard_map/ppermute | solution.py:41
  24.6 19.8 %copy-start.12 = (s32[8]{0:T(128)S(1)}, s32[8]{0:T(128)}, u32[]{:S(2)}) copy-start(s32[8]{0:T(128)} %constant.81.clone) | copy-start | bytes 100
  24.6 19.8 %copy-start.13 = (s32[8]{0:T(128)S(1)}, s32[8]{0:T(128)}, u32[]{:S(2)}) copy-start(s32[8]{0:T(128)} %constant.82.clone) | copy-start | bytes 100
  25.8 29.3 %collective-permute-start.5 = (bf16[2,784,384]{2,1,0:T(8,128)(2,1)}, bf16[2,784,384]{2,1,0:T(8,128)(2,1)}, u32[]{:S(2)}, u32[]{:S(2)}) collective-permute-start(bf16[2,784,384]{2,1,0:T(8,128)(2,1)} %pad_maximum_fusion), channel_id=1, source_target_pairs={{0,1},{1,2},{2,3},{3,0},{4,5},{5,6},{6,7},{7,4},{8,9},{9,10},{10,1... | collective-permute-start | bytes 3612680 | tf_op jit(solution)/shard_map/ppermute | solution.py:41
  37.3 17.7 %collective-permute-start.4 = (bf16[784,384]{1,0:T(8,128)(2,1)}, bf16[784,384]{1,0:T(8,128)(2,1)S(1)}, u32[]{:S(2)}, u32[]{:S(2)}) collective-permute-start(bf16[784,384]{1,0:T(8,128)(2,1)} %collective-permute-done.3.refs_0_.refs_4_), channel_id=1, source_target_pairs={{0,3},{1,0},{2,1},{3,2},{4,7},{5,4},{6,5},{7,6},{8,11},{9,8},{10,9... | collective-permute-start | bytes 1806344 | tf_op jit(solution)/shard_map/ppermute | solution.py:41
  40.0 35.2 %collective-permute-start.9 = (bf16[2,768,384]{2,1,0:T(8,128)(2,1)}, bf16[2,768,384]{2,1,0:T(8,128)(2,1)}, u32[]{:S(2)}, u32[]{:S(2)}) collective-permute-start(bf16[2,768,384]{2,1,0:T(8,128)(2,1)} %collective-permute-done.6.refs_4_), channel_id=1, source_target_pairs={{0,16},{8,24},{16,32},{24,40},{32,48},{40,56},{48,0},{56,8},{64,80... | collective-permute-start | bytes 3538952 | tf_op jit(solution)/shard_map/ppermute | solution.py:37
  41.5 35.7 %collective-permute-start.10 = (bf16[2,768,384]{2,1,0:T(8,128)(2,1)}, bf16[2,768,384]{2,1,0:T(8,128)(2,1)}, u32[]{:S(2)}, u32[]{:S(2)}) collective-permute-start(bf16[2,768,384]{2,1,0:T(8,128)(2,1)} %refs_3_.1), channel_id=1, source_target_pairs={{0,64},{8,72},{16,80},{24,88},{32,96},{40,104},{48,112},{56,120},{... | collective-permute-start | bytes 3538952 | tf_op jit(solution)/shard_map/ppermute | solution.py:37
  42.5 39.8 %collective-permute-start.8 = (bf16[2,768,384]{2,1,0:T(8,128)(2,1)}, bf16[2,768,384]{2,1,0:T(8,128)(2,1)}, u32[]{:S(2)}, u32[]{:S(2)}) collective-permute-start(bf16[2,768,384]{2,1,0:T(8,128)(2,1)} %refs_3_.1), channel_id=1, source_target_pairs={{0,48},{8,56},{16,0},{24,8},{32,16},{40,24},{48,32},{56,40},{64,11... | collective-permute-start | bytes 3538952 | tf_op jit(solution)/shard_map/ppermute | solution.py:37
  55.1 13.1 %slice-start = ((s8[7077888]{0:T(1024)(128)(4,1)}), s8[4194304]{0:T(1024)(128)(4,1)S(1)}, s32[]{:S(2)}) async-start(s8[7077888]{0:T(1024)(128)(4,1)} %bitcast.15), calls=%async_computation.4 | async-start | bytes 8388608
  55.9 12.3 %copy-start.1 = (s32[8]{0:T(128)S(1)}, s32[8]{0:T(128)}, u32[]{:S(2)}) copy-start(s32[8]{0:T(128)} %fusion.idx_ref) | copy-start | bytes 100
  55.9 12.3 %copy-start.2 = (f32[2,128]{1,0:T(2,128)S(1)}, f32[2,128]{1,0:T(2,128)}, u32[]{:S(2)}) copy-start(f32[2,128]{1,0:T(2,128)} %refs_9_.1) | copy-start | bytes 3076
  67.5 16.6 %collective-permute-start.7 = (bf16[768,384]{1,0:T(8,128)(2,1)}, bf16[768,384]{1,0:T(8,128)(2,1)S(1)}, u32[]{:S(2)}, u32[]{:S(2)}) collective-permute-start(bf16[768,384]{1,0:T(8,128)(2,1)} %get-tuple-element.31.refs_0_.q_ref), channel_id=1, source_target_pairs={{0,8},{8,0},{16,24},{24,16},{32,40},{40,32},{48,56},{56,48},{64,72... | collective-permute-start | bytes 1769480 | tf_op jit(solution)/shard_map/ppermute | solution.py:37
  71.2 36.5 %all-to-all-start = ((bf16[16,16,1152]{2,1,0:T(8,128)(2,1)}), bf16[16,16,1152]{2,1,0:T(8,128)(2,1)S(1)}, u32[]{:S(2)}, u32[]{:S(2)}) async-start(bf16[16,16,1152]{2,1,0:T(8,128)(2,1)} %broadcast_in_dim.4), calls=%async_computation | async-start | bytes 1179648 | tf_op jit(solution)/shard_map/all_to_all | solution.py:582
  75.3 36.3 %collective-permute-start.13 = (bf16[2,768,384]{2,1,0:T(8,128)(2,1)}, bf16[2,768,384]{2,1,0:T(8,128)(2,1)}, u32[]{:S(2)}, u32[]{:S(2)}) collective-permute-start(bf16[2,768,384]{2,1,0:T(8,128)(2,1)} %collective-permute-done.9.refs_6_), channel_id=1, source_target_pairs={{0,64},{8,72},{16,80},{24,88},{32,96},{40,104},{48,112},{56,120},{... | collective-permute-start | bytes 3538952 | tf_op jit(solution)/shard_map/ppermute | solution.py:37
  77.3 49.9 %collective-permute-start.15 = (bf16[192,1536]{1,0:T(8,128)(2,1)S(1)}, bf16[192,1536]{1,0:T(8,128)(2,1)S(1)}, u32[]{:S(2)}, u32[]{:S(2)}) collective-permute-start(bf16[192,1536]{1,0:T(8,128)(2,1)S(1)} %copy-done.10), channel_id=1, source_target_pairs={{0,4},{1,5},{2,6},{3,7},{4,0},{5,1},{6,2},{7,3},{8,12},{9,13},{10,... | collective-permute-start | bytes 1769480 | tf_op jit(solution)/shard_map/ppermute | solution.py:41
  80.8 30.7 %collective-permute-start.11 = (bf16[2,768,384]{2,1,0:T(8,128)(2,1)}, bf16[2,768,384]{2,1,0:T(8,128)(2,1)}, u32[]{:S(2)}, u32[]{:S(2)}) collective-permute-start(bf16[2,768,384]{2,1,0:T(8,128)(2,1)} %collective-permute-done.10.refs_7_), channel_id=1, source_target_pairs={{0,16},{8,24},{16,32},{24,40},{32,48},{40,56},{48,0},{56,8},{64,80... | collective-permute-start | bytes 3538952 | tf_op jit(solution)/shard_map/ppermute | solution.py:37
  82.3 29.3 %collective-permute-start.12 = (bf16[2,768,384]{2,1,0:T(8,128)(2,1)}, bf16[2,768,384]{2,1,0:T(8,128)(2,1)}, u32[]{:S(2)}, u32[]{:S(2)}) collective-permute-start(bf16[2,768,384]{2,1,0:T(8,128)(2,1)} %collective-permute-done.10.refs_7_), channel_id=1, source_target_pairs={{0,48},{8,56},{16,0},{24,8},{32,16},{40,24},{48,32},{56,40},{64,11... | collective-permute-start | bytes 3538952 | tf_op jit(solution)/shard_map/ppermute | solution.py:37
  127.0 4.9 %collective-permute-start.14 = (bf16[2,768,384]{2,1,0:T(8,128)(2,1)}, bf16[2,768,384]{2,1,0:T(8,128)(2,1)}, u32[]{:S(2)}, u32[]{:S(2)}) collective-permute-start(bf16[2,768,384]{2,1,0:T(8,128)(2,1)} %get-tuple-element.44), channel_id=1, source_target_pairs={{0,8},{8,0},{16,24},{24,16},{32,40},{40,32},{48,56},{56,48},{64,72... | collective-permute-start | bytes 3538952 | tf_op jit(solution)/shard_map/ppermute | solution.py:37
  127.2 4.7 %collective-permute-start.16 = (bf16[192,1536]{1,0:T(8,128)(2,1)S(1)}, bf16[192,1536]{1,0:T(8,128)(2,1)S(1)}, u32[]{:S(2)}, u32[]{:S(2)}) collective-permute-start(bf16[192,1536]{1,0:T(8,128)(2,1)S(1)} %collective-permute-done.15.wz_ref), channel_id=1, source_target_pairs={{0,8},{8,0},{16,24},{24,16},{32,40},{40,32},{48,56},{56,48},{64,72... | collective-permute-start | bytes 1769480 | tf_op jit(solution)/shard_map/ppermute | solution.py:37
  128.3 12.8 %all-to-all-start.1 = ((bf16[16,2,16,384]{3,2,1,0:T(8,128)(2,1)}), bf16[16,2,16,384]{3,2,1,0:T(8,128)(2,1)S(1)}, u32[]{:S(2)}, u32[]{:S(2)}) async-start(bf16[16,2,16,384]{3,2,1,0:T(8,128)(2,1)} %text_attention.1), calls=%async_computation.1 | async-start | bytes 786432 | tf_op jit(solution)/shard_map/all_to_all | solution.py:594
  136.2 19.2 %collective-permute-start.17 = (bf16[768,384]{1,0:T(8,128)(2,1)}, bf16[768,384]{1,0:T(8,128)(2,1)}, u32[]{:S(2)}, u32[]{:S(2)}) collective-permute-start(bf16[768,384]{1,0:T(8,128)(2,1)} %quotient.1.mine_ref), channel_id=1, source_target_pairs={{0,4},{1,5},{2,6},{3,7},{4,0},{5,1},{6,2},{7,3},{8,12},{9,13},{10,... | collective-permute-start | bytes 1769480 | tf_op jit(solution)/shard_map/ppermute | solution.py:41
  145.1 20.0 %all-to-all-start.2 = ((bf16[8,16,384]{2,1,0:T(8,128)(2,1)}), bf16[8,16,384]{2,1,0:T(8,128)(2,1)S(1)}, u32[]{:S(2)}, u32[]{:S(2)}) async-start(bf16[8,16,384]{2,1,0:T(8,128)(2,1)} %text_quotient.1), calls=%async_computation.2 | async-start | bytes 196608 | tf_op jit(solution)/shard_map/all_to_all | solution.py:612
  161.8 30.1 %copy-start.8 = (bf16[768,384]{1,0:T(8,128)(2,1)S(1)}, bf16[768,384]{1,0:T(8,128)(2,1)}, u32[]{:S(2)}) copy-start(bf16[768,384]{1,0:T(8,128)(2,1)} %param.14) | copy-start | bytes 1769476
  161.8 29.4 %collective-permute-start.18 = (bf16[768,384]{1,0:T(8,128)(2,1)}, bf16[768,384]{1,0:T(8,128)(2,1)S(1)}, u32[]{:S(2)}, u32[]{:S(2)}) collective-permute-start(bf16[768,384]{1,0:T(8,128)(2,1)} %get-tuple-element.48), channel_id=1, source_target_pairs={{0,1},{1,2},{2,3},{3,0},{4,5},{5,6},{6,7},{7,4},{8,9},{9,10},{10,1... | collective-permute-start | bytes 1769480 | tf_op jit(solution)/shard_map/ppermute | solution.py:41
  161.9 29.3 %collective-permute-start.19 = (bf16[768,384]{1,0:T(8,128)(2,1)}, bf16[768,384]{1,0:T(8,128)(2,1)S(1)}, u32[]{:S(2)}, u32[]{:S(2)}) collective-permute-start(bf16[768,384]{1,0:T(8,128)(2,1)} %get-tuple-element.49), channel_id=1, source_target_pairs={{0,2},{1,3},{2,0},{3,1},{4,6},{5,7},{6,4},{7,5},{8,10},{9,11},{10,... | collective-permute-start | bytes 1769480 | tf_op jit(solution)/shard_map/ppermute | solution.py:41
  163.4 28.4 %collective-permute-start.20 = (bf16[768,384]{1,0:T(8,128)(2,1)}, bf16[768,384]{1,0:T(8,128)(2,1)S(1)}, u32[]{:S(2)}, u32[]{:S(2)}) collective-permute-start(bf16[768,384]{1,0:T(8,128)(2,1)} %get-tuple-element.50), channel_id=1, source_target_pairs={{0,3},{1,0},{2,1},{3,2},{4,7},{5,4},{6,5},{7,6},{8,11},{9,8},{10,9... | collective-permute-start | bytes 1769480 | tf_op jit(solution)/shard_map/ppermute | solution.py:41
  166.6 11.4 %all-to-all-start.3 = ((bf16[16,16,384]{2,1,0:T(8,128)(2,1)}), bf16[16,16,384]{2,1,0:T(8,128)(2,1)S(1)}, u32[]{:S(2)}, u32[]{:S(2)}) async-start(bf16[16,16,384]{2,1,0:T(8,128)(2,1)} %broadcast_in_dim.5), calls=%async_computation.3 | async-start | bytes 393216 | tf_op jit(solution)/shard_map/all_to_all | solution.py:615
  (12 other events, 64.1 us)

commit v2 on v1

--- a/solution.py
+++ b/solution.py
@@ -407,27 +407,37 @@
     return one(q_ref[:, at : at + hd], k, v, len_ref[0])
 
 
-def image_quotient(len_ref, q_ref, txt_ref, num_ref, den_ref, got_ref, attn_ref):
+def image_quotient(len_ref, q_ref, k_ref, v_ref, num_ref, den_ref, got_ref, attn_ref):
+    n, d = one(q_ref[...], k_ref[...], v_ref[...], len_ref[0])
+    num = n + num_ref[...] + got_ref[0].astype(F32)
+    den = d + den_ref[...] + got_ref[1].astype(F32)
+    attn_ref[...] = (num / den).astype(BF)
+
+
+def quotient(text_len, q, txt, num, den, got):
+    rows, width = q.shape
+    keys = txt.shape[0]
     hd = 128
-    for h in range(num_ref.shape[1] // hd):
-        cols = slice(h * hd, (h + 1) * hd)
-        n, d = text_keys(q_ref, txt_ref, len_ref, h)
-        num = n + num_ref[:, cols] + got_ref[0, :, cols].astype(F32)
-        den = d + den_ref[:, cols] + got_ref[1, :, cols].astype(F32)
-        attn_ref[:, cols] = (num / den).astype(BF)
-
-
-def quotient(text_len, q, txt, num, den, got):
-    vmem = pl.BlockSpec(memory_space=pltpu.VMEM)
+    heads = width // hd
+    part = pl.BlockSpec((rows, hd), lambda h: (0, h))
     return pl.pallas_call(
         image_quotient,
-        in_specs=[pl.BlockSpec(memory_space=pltpu.SMEM)] + [vmem] * 5,
-        out_specs=vmem,
+        grid=(heads,),
+        in_specs=[
+            pl.BlockSpec(memory_space=pltpu.SMEM),
+            part,
+            pl.BlockSpec((keys, hd), lambda h: (0, heads + h)),
+            pl.BlockSpec((keys, hd), lambda h: (0, 2 * heads + h)),
+            part,
+            part,
+            pl.BlockSpec((2, rows, hd), lambda h: (0, 0, h)),
+        ],
+        out_specs=part,
         out_shape=jax.ShapeDtypeStruct(q.shape, BF),
         compiler_params=pltpu.CompilerParams(vmem_limit_bytes=VMEM),
         cost_estimate=cost(4),
         name="quotient",
-    )(text_len, q, txt, num, den, got)
+    )(text_len, q, txt, txt, num, den, got)
 
 
 def text_quotient_kernel(len_ref, sum_ref, q_ref, txt_ref, proj_ref, out_ref):

time: 196 us -> 196 us (level)
  no operation moved by 1% of the time
where the time goes in v2:
time: 196 us; the launch traced here: 195 us
  Pallas kernels  79.5 us (41%)
  starting transfers between devices  51.5 us (26%)
  waiting for transfers between devices  46 us (23%)
  local copies, waits for them, and re-layouts  9.67 us (5%)
  other arithmetic  6.6 us (3%)
    ppermute x11, waiting for transfers between devices, send_head(): return lax.ppermute(x, 'head', head_perm(dz, dy))  39.5 us
    pallas_call x2, Pallas kernels, attention(): pl.pallas_call(functools.partial(att_kernel, plan=plan, n_q=n_q, n_kv=len...  38.2 us
    ppermute x11, starting transfers between devices, send_head(): return lax.ppermute(x, 'head', head_perm(dz, dy))  22.5 us
    ppermute x10, starting transfers between devices, send_patch(): return lax.ppermute(x, 'patch', patch_perm(dz, dx, dc))  11.8 us
    pallas_call x1, Pallas kernels, late_qkv(): pl.pallas_call(functools.partial(late_kernel, first=first, tile=tile, sca...  11.5 us
    pallas_call x1, Pallas kernels, early_qkv(): pl.pallas_call(functools.partial(early_kernel, blocks=n, rows=rows), in_s...  10.1 us
    pallas_call x1, Pallas kernels, project(): pl.pallas_call(proj_kernel, in_specs=[pl.BlockSpec(memory_space=pltpu.SME...  6.38 us
    all_to_all x1, waiting for transfers between devices, shards(): lax.all_to_all(jnp.broadcast_to(t_out[None], (n_patch,) + t_out.shape), '...  6.26 us
  transfers between devices with their start and end apart: 25, of which 8 were waited for; matrix products, arithmetic and copies ran while one was open for 4% of the time, Pallas kernels for 41%

profile of v2, /device:TPU:0, one launch (start us, length us, event | category | flops | bytes accessed | tf_op | source)
XLA Modules:
  0.0 194.8 jit_solution(5335156562133276803)
XLA Ops:
  2.5 1.7 collective-permute-start.1
  4.2 1.6 collective-permute-start.2
  5.8 4.0 %collective-permute-start = (bf16[784,384]{1,0:T(8,128)(2,1)S(1)}, bf16[784,384]{1,0:T(8,128)(2,1)S(1)}, u32[]{:S(2)}, u32[]{:S(2)}) collective-permute-start(bf16[784,384]{1,0:T(8,128)(2,1)S(1)} %pad_maximum_fusion.1.refs_0_), channel_id=1, source_target_pairs={{0,4},{1,5},{2,6},{3,7},{4,0},{5,1},{6,2},{7,3},{8,12},{9,13},{10,... | collective-permute-start | bytes 1806344 | tf_op jit(solution)/shard_map/ppermute | solution.py:41
  11.2 2.0 %dynamic_slice.14 = bf16[192,1536]{1,0:T(8,128)(2,1)} dynamic-slice(bf16[384,3072]{1,0:T(8,128)(2,1)} %w_ref.1, s32[]{:T(128)S(6)} %select_n.47, s32[]{:T(128)S(6)} %select_n.48), dynamic_slice_sizes={192,1536} | dynamic-slice | bytes 1179652 | tf_op jit(solution)/shard_map/dynamic_slice | solution.py:564
  13.2 6.0 %collective-permute-done.1.refs_2_ = bf16[784,384]{1,0:T(8,128)(2,1)S(1)} collective-permute-done((bf16[784,384]{1,0:T(8,128)(2,1)S(1)}, bf16[784,384]{1,0:T(8,128)(2,1)S(1)}, u32[]{:S(2)}, u32[]{:S(2)}) %collective-permute-start.1) | collective-permute-done | bytes 602144 | tf_op jit(solution)/shard_map/ppermute | solution.py:41
  19.3 3.7 %collective-permute-done.refs_1_ = bf16[784,384]{1,0:T(8,128)(2,1)S(1)} collective-permute-done((bf16[784,384]{1,0:T(8,128)(2,1)S(1)}, bf16[784,384]{1,0:T(8,128)(2,1)S(1)}, u32[]{:S(2)}, u32[]{:S(2)}) %collective-permute-start) | collective-permute-done | bytes 602144 | tf_op jit(solution)/shard_map/ppermute | solution.py:41
  22.9 1.7 collective-permute-start.3
  26.2 11.1 %collective-permute-done.3.refs_0_.refs_4_ = bf16[784,384]{1,0:T(8,128)(2,1)} collective-permute-done((bf16[784,384]{1,0:T(8,128)(2,1)S(1)}, bf16[784,384]{1,0:T(8,128)(2,1)}, u32[]{:S(2)}, u32[]{:S(2)}) %collective-permute-start.3) | collective-permute-done | bytes 602144 | tf_op jit(solution)/shard_map/ppermute | solution.py:41
  37.3 2.7 %collective-permute-start.4 = (bf16[784,384]{1,0:T(8,128)(2,1)}, bf16[784,384]{1,0:T(8,128)(2,1)S(1)}, u32[]{:S(2)}, u32[]{:S(2)}) collective-permute-start(bf16[784,384]{1,0:T(8,128)(2,1)} %collective-permute-done.3.refs_0_.refs_4_), channel_id=1, source_target_pairs={{0,3},{1,0},{2,1},{3,2},{4,7},{5,4},{6,5},{7,6},{8,11},{9,8},{10,9... | collective-permute-start | bytes 1806344 | tf_op jit(solution)/shard_map/ppermute | solution.py:41
  42.5 1.9 collective-permute-start.8
  45.0 10.1 %early_qkv.1 = (f32[784,1152]{1,0:T(8,128)}, f32[2,768,128]{2,1,0:T(8,128)}) custom-call(s32[8]{0:T(128)} %fusion.idx_ref, bf16[784,384]{1,0:T(8,128)(2,1)} %copy-done.3, bf16[784,384]{1,0:T(8,128)(2,1)} %copy-done.5, bf16[784,384]{1,0:T(8,128)(2,1)} %copy-done.4, bf16[784,384]{1,0:T(8,128)(2,1)} %copy-done.6, bf16[3,3072,384]{2,1,0:T(8,128)(2,1)} %bitcast.19, ...), custom_call_target="tpu_custom_call" | custom-call | flops 1 | bytes 1 | tf_op jit(solution)/shard_map/early_qkv/pallas_call | solution.py:195
  55.9 11.5 %late_qkv.1 = (bf16[768,384]{1,0:T(8,128)(2,1)}, bf16[2,768,384]{2,1,0:T(8,128)(2,1)}) custom-call(s32[8]{0:T(128)} %fusion.idx_ref, bf16[784,384]{1,0:T(8,128)(2,1)} %collective-permute-done.3.refs_0_.refs_4_, bf16[784,384]{1,0:T(8,128)(2,1)} %copy-done.7, bf16[2,784,384]{2,1,0:T(8,128)(2,1)} %collective-permute-done.5.refs_2_.refs_6_, ...), custom_call_target="tpu_custom_call" | custom-call | flops 1 | bytes 1 | tf_op jit(solution)/shard_map/late_qkv/pallas_call | solution.py:223
  68.3 2.1 %text_qkv.1 = bf16[16,1152]{1,0:T(8,128)(2,1)S(1)} custom-call(s32[8]{0:T(128)S(1)} %copy-done.1, bf16[784,384]{1,0:T(8,128)(2,1)} %copy-done.3, bf16[784,384]{1,0:T(8,128)(2,1)} %copy-done.5, bf16[784,384]{1,0:T(8,128)(2,1)} %copy-done.4, bf16[784,384]{1,0:T(8,128)(2,1)} %copy-done.6, bf16[784,384]{1,0:T(8,128)(2,1)} %collective-permute-done.3.refs_0_.refs_4_, ...), custom_call_target="tpu_custom_call" | custom-call | flops 2300000000 | bytes 1 | tf_op jit(solution)/shard_map/text_qkv/pallas_call | solution.py:270
  71.2 4.0 %all-to-all-start = ((bf16[16,16,1152]{2,1,0:T(8,128)(2,1)}), bf16[16,16,1152]{2,1,0:T(8,128)(2,1)S(1)}, u32[]{:S(2)}, u32[]{:S(2)}) async-start(bf16[16,16,1152]{2,1,0:T(8,128)(2,1)} %broadcast_in_dim.4), calls=%async_computation | async-start | bytes 1179648 | tf_op jit(solution)/shard_map/all_to_all | solution.py:592
  75.3 2.0 %collective-permute-start.13 = (bf16[2,768,384]{2,1,0:T(8,128)(2,1)}, bf16[2,768,384]{2,1,0:T(8,128)(2,1)}, u32[]{:S(2)}, u32[]{:S(2)}) collective-permute-start(bf16[2,768,384]{2,1,0:T(8,128)(2,1)} %collective-permute-done.9.refs_6_), channel_id=1, source_target_pairs={{0,64},{8,72},{16,80},{24,88},{32,96},{40,104},{48,112},{56,120},{... | collective-permute-start | bytes 3538952 | tf_op jit(solution)/shard_map/ppermute | solution.py:37
  77.3 3.6 %collective-permute-start.15 = (bf16[192,1536]{1,0:T(8,128)(2,1)S(1)}, bf16[192,1536]{1,0:T(8,128)(2,1)S(1)}, u32[]{:S(2)}, u32[]{:S(2)}) collective-permute-start(bf16[192,1536]{1,0:T(8,128)(2,1)S(1)} %copy-done.10), channel_id=1, source_target_pairs={{0,4},{1,5},{2,6},{3,7},{4,0},{5,1},{6,2},{7,3},{8,12},{9,13},{10,... | collective-permute-start | bytes 1769480 | tf_op jit(solution)/shard_map/ppermute | solution.py:41
  82.3 1.8 collective-permute-start.12
  84.9 22.8 %att_near.1 = (f32[768,384]{1,0:T(8,128)}, f32[768,384]{1,0:T(8,128)}, f32[768,384]{1,0:T(8,128)}, f32[768,384]{1,0:T(8,128)}) custom-call(s32[3]{0:T(128)} %pad_add_fusion.pos_ref, bf16[768,384]{1,0:T(8,128)(2,1)} %get-tuple-element.31.refs_0_.q_ref, bf16[768,384]{1,0:T(8,128)(2,1)} %copy-done.15, bf16[2,768,384]{2,1,0:T(8,128)(2,1)} %get-tuple-element.34.refs_2_.kv_ref, ...), custom_call_target="tpu_custom_call" | custom-call | flops 31708938240 | bytes 1 | tf_op jit(solution)/shard_map/att_near/pallas_call | solution.py:360
  108.5 3.0 %text_attention.1 = bf16[16,2,16,384]{3,2,1,0:T(8,128)(2,1)} custom-call(bf16[256,1152]{1,0:T(8,128)(2,1)} %bitcast.24, bf16[2,768,384]{2,1,0:T(8,128)(2,1)} %get-tuple-element.34.refs_2_.kv_ref), custom_call_target="tpu_custom_call" | custom-call | flops 3449999872 | bytes 1 | tf_op jit(solution)/shard_map/text_attention/pallas_call | solution.py:389
  111.6 15.4 %att_last.1 = (f32[768,384]{1,0:T(8,128)}, f32[768,384]{1,0:T(8,128)}, bf16[2,768,384]{2,1,0:T(8,128)(2,1)}) custom-call(s32[3]{0:T(128)} %pad_add_fusion.pos_ref, bf16[768,384]{1,0:T(8,128)(2,1)} %get-tuple-element.31.refs_0_.q_ref, bf16[768,384]{1,0:T(8,128)(2,1)} %copy-done.15, bf16[2,768,384]{2,1,0:T(8,128)(2,1)} %collective-permute-done.11.refs_2_, ...), custom_call_target="tpu_custom_call" | custom-call | flops 19025362944 | bytes 1 | tf_op jit(solution)/shard_map/att_last/pallas_call | solution.py:360
  128.3 3.6 %all-to-all-start.1 = ((bf16[16,2,16,384]{3,2,1,0:T(8,128)(2,1)}), bf16[16,2,16,384]{3,2,1,0:T(8,128)(2,1)S(1)}, u32[]{:S(2)}, u32[]{:S(2)}) async-start(bf16[16,2,16,384]{3,2,1,0:T(8,128)(2,1)} %text_attention.1), calls=%async_computation.1 | async-start | bytes 786432 | tf_op jit(solution)/shard_map/all_to_all | solution.py:604
  131.9 4.8 %quotient.1.mine_ref = bf16[768,384]{1,0:T(8,128)(2,1)} custom-call(s32[1]{0:T(128)S(6)} %copy.17.len_ref, bf16[768,384]{1,0:T(8,128)(2,1)} %get-tuple-element.31.refs_0_.q_ref, bf16[256,1152]{1,0:T(8,128)(2,1)} %bitcast.25, bf16[256,1152]{1,0:T(8,128)(2,1)} %bitcast.26, f32[768,384]{1,0:T(8,128)} %get-tuple-element.42.num_ref, ...), custom_call_target="tpu_custom_call" | custom-call | flops 4600000000 | bytes 1 | tf_op jit(solution)/shard_map/quotient/pallas_call | solution.py:423
  136.7 3.5 %collective-permute-start.17 = (bf16[768,384]{1,0:T(8,128)(2,1)}, bf16[768,384]{1,0:T(8,128)(2,1)}, u32[]{:S(2)}, u32[]{:S(2)}) collective-permute-start(bf16[768,384]{1,0:T(8,128)(2,1)} %quotient.1.mine_ref), channel_id=1, source_target_pairs={{0,4},{1,5},{2,6},{3,7},{4,0},{5,1},{6,2},{7,3},{8,12},{9,13},{10,... | collective-permute-start | bytes 1769480 | tf_op jit(solution)/shard_map/ppermute | solution.py:41
  141.8 3.4 %text_quotient.1 = bf16[8,16,384]{2,1,0:T(8,128)(2,1)} custom-call(s32[1]{0:T(128)S(6)} %copy.17.len_ref, bf16[16,2,16,384]{3,2,1,0:T(8,128)(2,1)} %copy-done.11, bf16[16,384]{1,0:T(8,128)(2,1)} %slice.12.q_ref, bf16[256,1152]{1,0:T(8,128)(2,1)} %bitcast.27, bf16[384,3072]{1,0:T(8,128)(2,1)} %proj_ref.1), custom_call_target="tpu_custom_call" | custom-call | flops 4600000000 | bytes 1 | tf_op jit(solution)/shard_map/text_quotient/pallas_call | solution.py:461
  145.1 4.8 %all-to-all-start.2 = ((bf16[8,16,384]{2,1,0:T(8,128)(2,1)}), bf16[8,16,384]{2,1,0:T(8,128)(2,1)S(1)}, u32[]{:S(2)}, u32[]{:S(2)}) async-start(bf16[8,16,384]{2,1,0:T(8,128)(2,1)} %text_quotient.1), calls=%async_computation.2 | async-start | bytes 196608 | tf_op jit(solution)/shard_map/all_to_all | solution.py:622
  150.0 5.5 %collective-permute-done.17.got_ref = bf16[768,384]{1,0:T(8,128)(2,1)} collective-permute-done((bf16[768,384]{1,0:T(8,128)(2,1)}, bf16[768,384]{1,0:T(8,128)(2,1)}, u32[]{:S(2)}, u32[]{:S(2)}) %collective-permute-start.17) | collective-permute-done | bytes 589856 | tf_op jit(solution)/shard_map/ppermute | solution.py:41
  155.5 6.4 %project.1 = (bf16[768,384]{1,0:T(8,128)(2,1)}, bf16[768,384]{1,0:T(8,128)(2,1)}, bf16[768,384]{1,0:T(8,128)(2,1)}, bf16[768,384]{1,0:T(8,128)(2,1)}) custom-call(s32[3]{0:T(128)} %pad_add_fusion.pos_ref, bf16[768,384]{1,0:T(8,128)(2,1)} %quotient.1.mine_ref, bf16[768,384]{1,0:T(8,128)(2,1)} %collective-permute-done.17.got_ref, bf16[384,3072]{1,0:T(8,128)(2,1)} %w_ref.1, ...), custom_call_target="tpu_custom_call" | custom-call | flops 6899999744 | bytes 1 | tf_op jit(solution)/shard_map/project/pallas_call | solution.py:510
  163.4 1.8 collective-permute-start.20
  166.7 4.8 %all-to-all-start.3 = ((bf16[16,16,384]{2,1,0:T(8,128)(2,1)}), bf16[16,16,384]{2,1,0:T(8,128)(2,1)S(1)}, u32[]{:S(2)}, u32[]{:S(2)}) async-start(bf16[16,16,384]{2,1,0:T(8,128)(2,1)} %broadcast_in_dim.5), calls=%async_computation.3 | async-start | bytes 393216 | tf_op jit(solution)/shard_map/all_to_all | solution.py:625
  172.4 6.3 %all-to-all-done.3 = bf16[16,16,384]{2,1,0:T(8,128)(2,1)S(1)} async-done(((bf16[16,16,384]{2,1,0:T(8,128)(2,1)}), bf16[16,16,384]{2,1,0:T(8,128)(2,1)S(1)}, u32[]{:S(2)}, u32[]{:S(2)}) %all-to-all-start.3) | async-done | bytes 196640 | tf_op jit(solution)/shard_map/all_to_all | solution.py:625
  178.6 12.5 %collective-permute-done.18 = bf16[768,384]{1,0:T(8,128)(2,1)S(1)} collective-permute-done((bf16[768,384]{1,0:T(8,128)(2,1)}, bf16[768,384]{1,0:T(8,128)(2,1)S(1)}, u32[]{:S(2)}, u32[]{:S(2)}) %collective-permute-start.18) | collective-permute-done | bytes 589856 | tf_op jit(solution)/shard_map/ppermute | solution.py:41
  191.8 2.3 %add_convert_fusion = bf16[768,384]{1,0:T(8,128)(2,1)} fusion(bf16[768,384]{1,0:T(8,128)(2,1)S(1)} %collective-permute-done.20, bf16[768,384]{1,0:T(8,128)(2,1)S(1)} %collective-permute-done.19, bf16[768,384]{1,0:T(8,128)(2,1)S(1)} %collective-permute-done.18, bf16[768,384]{1,0:T(8,128)(2,1)} %get-tuple-element.47, bf16[768,384]{1,0:T(8,128)(2,1)S(1)} %copy-done.8, ...), kind=kLoop, calls=%fused_computation.1 | loop fusion | flops 3244032 | bytes 3540480 | tf_op jit(solution)/shard_map/convert_element_type | solution.py:621
  (83 shorter events, 21.0 us)
Async XLA Ops:
  2.5 23.3 %copy-start.3 = (bf16[784,384]{1,0:T(8,128)(2,1)}, bf16[784,384]{1,0:T(8,128)(2,1)S(1)}, u32[]{:S(2)}) copy-start(bf16[784,384]{1,0:T(8,128)(2,1)S(1)} %pad_maximum_fusion.1.refs_0_) | copy-start | bytes 1806340
  2.5 16.8 %collective-permute-start.1 = (bf16[784,384]{1,0:T(8,128)(2,1)S(1)}, bf16[784,384]{1,0:T(8,128)(2,1)S(1)}, u32[]{:S(2)}, u32[]{:S(2)}) collective-permute-start(bf16[784,384]{1,0:T(8,128)(2,1)S(1)} %pad_maximum_fusion.1.refs_0_), channel_id=1, source_target_pairs={{0,1},{1,2},{2,3},{3,0},{4,5},{5,6},{6,7},{7,4},{8,9},{9,10},{10,1... | collective-permute-start | bytes 1806344 | tf_op jit(solution)/shard_map/ppermute | solution.py:41
  4.2 15.1 %collective-permute-start.2 = (bf16[784,384]{1,0:T(8,128)(2,1)S(1)}, bf16[784,384]{1,0:T(8,128)(2,1)S(1)}, u32[]{:S(2)}, u32[]{:S(2)}) collective-permute-start(bf16[784,384]{1,0:T(8,128)(2,1)S(1)} %pad_maximum_fusion.1.refs_0_), channel_id=1, source_target_pairs={{0,3},{1,0},{2,1},{3,2},{4,7},{5,4},{6,5},{7,6},{8,11},{9,8},{10,9... | collective-permute-start | bytes 1806344 | tf_op jit(solution)/shard_map/ppermute | solution.py:41
  5.8 17.1 %collective-permute-start = (bf16[784,384]{1,0:T(8,128)(2,1)S(1)}, bf16[784,384]{1,0:T(8,128)(2,1)S(1)}, u32[]{:S(2)}, u32[]{:S(2)}) collective-permute-start(bf16[784,384]{1,0:T(8,128)(2,1)S(1)} %pad_maximum_fusion.1.refs_0_), channel_id=1, source_target_pairs={{0,4},{1,5},{2,6},{3,7},{4,0},{5,1},{6,2},{7,3},{8,12},{9,13},{10,... | collective-permute-start | bytes 1806344 | tf_op jit(solution)/shard_map/ppermute | solution.py:41
  9.8 30.3 %collective-permute-start.6 = (bf16[2,768,384]{2,1,0:T(8,128)(2,1)}, bf16[2,768,384]{2,1,0:T(8,128)(2,1)}, u32[]{:S(2)}, u32[]{:S(2)}) collective-permute-start(bf16[2,768,384]{2,1,0:T(8,128)(2,1)} %refs_3_.1), channel_id=1, source_target_pairs={{0,16},{8,24},{16,32},{24,40},{32,48},{40,56},{48,0},{56,8},{64,80... | collective-permute-start | bytes 3538952 | tf_op jit(solution)/shard_map/ppermute | solution.py:37
  22.9 14.4 %collective-permute-start.3 = (bf16[784,384]{1,0:T(8,128)(2,1)S(1)}, bf16[784,384]{1,0:T(8,128)(2,1)}, u32[]{:S(2)}, u32[]{:S(2)}) collective-permute-start(bf16[784,384]{1,0:T(8,128)(2,1)S(1)} %collective-permute-done.refs_1_), channel_id=1, source_target_pairs={{0,3},{1,0},{2,1},{3,2},{4,7},{5,4},{6,5},{7,6},{8,11},{9,8},{10,9... | collective-permute-start | bytes 1806344 | tf_op jit(solution)/shard_map/ppermute | solution.py:41
  24.6 19.8 %copy-start.12 = (s32[8]{0:T(128)S(1)}, s32[8]{0:T(128)}, u32[]{:S(2)}) copy-start(s32[8]{0:T(128)} %constant.81.clone) | copy-start | bytes 100
  24.6 19.8 %copy-start.13 = (s32[8]{0:T(128)S(1)}, s32[8]{0:T(128)}, u32[]{:S(2)}) copy-start(s32[8]{0:T(128)} %constant.82.clone) | copy-start | bytes 100
  25.8 29.3 %collective-permute-start.5 = (bf16[2,784,384]{2,1,0:T(8,128)(2,1)}, bf16[2,784,384]{2,1,0:T(8,128)(2,1)}, u32[]{:S(2)}, u32[]{:S(2)}) collective-permute-start(bf16[2,784,384]{2,1,0:T(8,128)(2,1)} %pad_maximum_fusion), channel_id=1, source_target_pairs={{0,1},{1,2},{2,3},{3,0},{4,5},{5,6},{6,7},{7,4},{8,9},{9,10},{10,1... | collective-permute-start | bytes 3612680 | tf_op jit(solution)/shard_map/ppermute | solution.py:41
  37.3 17.7 %collective-permute-start.4 = (bf16[784,384]{1,0:T(8,128)(2,1)}, bf16[784,384]{1,0:T(8,128)(2,1)S(1)}, u32[]{:S(2)}, u32[]{:S(2)}) collective-permute-start(bf16[784,384]{1,0:T(8,128)(2,1)} %collective-permute-done.3.refs_0_.refs_4_), channel_id=1, source_target_pairs={{0,3},{1,0},{2,1},{3,2},{4,7},{5,4},{6,5},{7,6},{8,11},{9,8},{10,9... | collective-permute-start | bytes 1806344 | tf_op jit(solution)/shard_map/ppermute | solution.py:41
  40.0 35.2 %collective-permute-start.9 = (bf16[2,768,384]{2,1,0:T(8,128)(2,1)}, bf16[2,768,384]{2,1,0:T(8,128)(2,1)}, u32[]{:S(2)}, u32[]{:S(2)}) collective-permute-start(bf16[2,768,384]{2,1,0:T(8,128)(2,1)} %collective-permute-done.6.refs_4_), channel_id=1, source_target_pairs={{0,16},{8,24},{16,32},{24,40},{32,48},{40,56},{48,0},{56,8},{64,80... | collective-permute-start | bytes 3538952 | tf_op jit(solution)/shard_map/ppermute | solution.py:37
  41.5 35.7 %collective-permute-start.10 = (bf16[2,768,384]{2,1,0:T(8,128)(2,1)}, bf16[2,768,384]{2,1,0:T(8,128)(2,1)}, u32[]{:S(2)}, u32[]{:S(2)}) collective-permute-start(bf16[2,768,384]{2,1,0:T(8,128)(2,1)} %refs_3_.1), channel_id=1, source_target_pairs={{0,64},{8,72},{16,80},{24,88},{32,96},{40,104},{48,112},{56,120},{... | collective-permute-start | bytes 3538952 | tf_op jit(solution)/shard_map/ppermute | solution.py:37
  42.5 39.8 %collective-permute-start.8 = (bf16[2,768,384]{2,1,0:T(8,128)(2,1)}, bf16[2,768,384]{2,1,0:T(8,128)(2,1)}, u32[]{:S(2)}, u32[]{:S(2)}) collective-permute-start(bf16[2,768,384]{2,1,0:T(8,128)(2,1)} %refs_3_.1), channel_id=1, source_target_pairs={{0,48},{8,56},{16,0},{24,8},{32,16},{40,24},{48,32},{56,40},{64,11... | collective-permute-start | bytes 3538952 | tf_op jit(solution)/shard_map/ppermute | solution.py:37
  55.1 13.1 %slice-start = ((s8[7077888]{0:T(1024)(128)(4,1)}), s8[4194304]{0:T(1024)(128)(4,1)S(1)}, s32[]{:S(2)}) async-start(s8[7077888]{0:T(1024)(128)(4,1)} %bitcast.15), calls=%async_computation.4 | async-start | bytes 8388608
  55.9 12.3 %copy-start.1 = (s32[8]{0:T(128)S(1)}, s32[8]{0:T(128)}, u32[]{:S(2)}) copy-start(s32[8]{0:T(128)} %fusion.idx_ref) | copy-start | bytes 100
  55.9 12.3 %copy-start.2 = (f32[2,128]{1,0:T(2,128)S(1)}, f32[2,128]{1,0:T(2,128)}, u32[]{:S(2)}) copy-start(f32[2,128]{1,0:T(2,128)} %refs_9_.1) | copy-start | bytes 3076
  67.5 16.6 %collective-permute-start.7 = (bf16[768,384]{1,0:T(8,128)(2,1)}, bf16[768,384]{1,0:T(8,128)(2,1)S(1)}, u32[]{:S(2)}, u32[]{:S(2)}) collective-permute-start(bf16[768,384]{1,0:T(8,128)(2,1)} %get-tuple-element.31.refs_0_.q_ref), channel_id=1, source_target_pairs={{0,8},{8,0},{16,24},{24,16},{32,40},{40,32},{48,56},{56,48},{64,72... | collective-permute-start | bytes 1769480 | tf_op jit(solution)/shard_map/ppermute | solution.py:37
  71.2 36.5 %all-to-all-start = ((bf16[16,16,1152]{2,1,0:T(8,128)(2,1)}), bf16[16,16,1152]{2,1,0:T(8,128)(2,1)S(1)}, u32[]{:S(2)}, u32[]{:S(2)}) async-start(bf16[16,16,1152]{2,1,0:T(8,128)(2,1)} %broadcast_in_dim.4), calls=%async_computation | async-start | bytes 1179648 | tf_op jit(solution)/shard_map/all_to_all | solution.py:592
  75.3 36.3 %collective-permute-start.13 = (bf16[2,768,384]{2,1,0:T(8,128)(2,1)}, bf16[2,768,384]{2,1,0:T(8,128)(2,1)}, u32[]{:S(2)}, u32[]{:S(2)}) collective-permute-start(bf16[2,768,384]{2,1,0:T(8,128)(2,1)} %collective-permute-done.9.refs_6_), channel_id=1, source_target_pairs={{0,64},{8,72},{16,80},{24,88},{32,96},{40,104},{48,112},{56,120},{... | collective-permute-start | bytes 3538952 | tf_op jit(solution)/shard_map/ppermute | solution.py:37
  77.3 49.9 %collective-permute-start.15 = (bf16[192,1536]{1,0:T(8,128)(2,1)S(1)}, bf16[192,1536]{1,0:T(8,128)(2,1)S(1)}, u32[]{:S(2)}, u32[]{:S(2)}) collective-permute-start(bf16[192,1536]{1,0:T(8,128)(2,1)S(1)} %copy-done.10), channel_id=1, source_target_pairs={{0,4},{1,5},{2,6},{3,7},{4,0},{5,1},{6,2},{7,3},{8,12},{9,13},{10,... | collective-permute-start | bytes 1769480 | tf_op jit(solution)/shard_map/ppermute | solution.py:41
  80.8 30.7 %collective-permute-start.11 = (bf16[2,768,384]{2,1,0:T(8,128)(2,1)}, bf16[2,768,384]{2,1,0:T(8,128)(2,1)}, u32[]{:S(2)}, u32[]{:S(2)}) collective-permute-start(bf16[2,768,384]{2,1,0:T(8,128)(2,1)} %collective-permute-done.10.refs_7_), channel_id=1, source_target_pairs={{0,16},{8,24},{16,32},{24,40},{32,48},{40,56},{48,0},{56,8},{64,80... | collective-permute-start | bytes 3538952 | tf_op jit(solution)/shard_map/ppermute | solution.py:37
  82.3 29.3 %collective-permute-start.12 = (bf16[2,768,384]{2,1,0:T(8,128)(2,1)}, bf16[2,768,384]{2,1,0:T(8,128)(2,1)}, u32[]{:S(2)}, u32[]{:S(2)}) collective-permute-start(bf16[2,768,384]{2,1,0:T(8,128)(2,1)} %collective-permute-done.10.refs_7_), channel_id=1, source_target_pairs={{0,48},{8,56},{16,0},{24,8},{32,16},{40,24},{48,32},{56,40},{64,11... | collective-permute-start | bytes 3538952 | tf_op jit(solution)/shard_map/ppermute | solution.py:37
  127.0 4.9 %collective-permute-start.14 = (bf16[2,768,384]{2,1,0:T(8,128)(2,1)}, bf16[2,768,384]{2,1,0:T(8,128)(2,1)}, u32[]{:S(2)}, u32[]{:S(2)}) collective-permute-start(bf16[2,768,384]{2,1,0:T(8,128)(2,1)} %get-tuple-element.44), channel_id=1, source_target_pairs={{0,8},{8,0},{16,24},{24,16},{32,40},{40,32},{48,56},{56,48},{64,72... | collective-permute-start | bytes 3538952 | tf_op jit(solution)/shard_map/ppermute | solution.py:37
  127.2 4.7 %collective-permute-start.16 = (bf16[192,1536]{1,0:T(8,128)(2,1)S(1)}, bf16[192,1536]{1,0:T(8,128)(2,1)S(1)}, u32[]{:S(2)}, u32[]{:S(2)}) collective-permute-start(bf16[192,1536]{1,0:T(8,128)(2,1)S(1)} %collective-permute-done.15.wz_ref), channel_id=1, source_target_pairs={{0,8},{8,0},{16,24},{24,16},{32,40},{40,32},{48,56},{56,48},{64,72... | collective-permute-start | bytes 1769480 | tf_op jit(solution)/shard_map/ppermute | solution.py:37
  128.3 12.8 %all-to-all-start.1 = ((bf16[16,2,16,384]{3,2,1,0:T(8,128)(2,1)}), bf16[16,2,16,384]{3,2,1,0:T(8,128)(2,1)S(1)}, u32[]{:S(2)}, u32[]{:S(2)}) async-start(bf16[16,2,16,384]{3,2,1,0:T(8,128)(2,1)} %text_attention.1), calls=%async_computation.1 | async-start | bytes 786432 | tf_op jit(solution)/shard_map/all_to_all | solution.py:604
  136.7 18.8 %collective-permute-start.17 = (bf16[768,384]{1,0:T(8,128)(2,1)}, bf16[768,384]{1,0:T(8,128)(2,1)}, u32[]{:S(2)}, u32[]{:S(2)}) collective-permute-start(bf16[768,384]{1,0:T(8,128)(2,1)} %quotient.1.mine_ref), channel_id=1, source_target_pairs={{0,4},{1,5},{2,6},{3,7},{4,0},{5,1},{6,2},{7,3},{8,12},{9,13},{10,... | collective-permute-start | bytes 1769480 | tf_op jit(solution)/shard_map/ppermute | solution.py:41
  145.1 20.1 %all-to-all-start.2 = ((bf16[8,16,384]{2,1,0:T(8,128)(2,1)}), bf16[8,16,384]{2,1,0:T(8,128)(2,1)S(1)}, u32[]{:S(2)}, u32[]{:S(2)}) async-start(bf16[8,16,384]{2,1,0:T(8,128)(2,1)} %text_quotient.1), calls=%async_computation.2 | async-start | bytes 196608 | tf_op jit(solution)/shard_map/all_to_all | solution.py:622
  161.9 29.9 %copy-start.8 = (bf16[768,384]{1,0:T(8,128)(2,1)S(1)}, bf16[768,384]{1,0:T(8,128)(2,1)}, u32[]{:S(2)}) copy-start(bf16[768,384]{1,0:T(8,128)(2,1)} %param.14) | copy-start | bytes 1769476
  161.9 29.3 %collective-permute-start.18 = (bf16[768,384]{1,0:T(8,128)(2,1)}, bf16[768,384]{1,0:T(8,128)(2,1)S(1)}, u32[]{:S(2)}, u32[]{:S(2)}) collective-permute-start(bf16[768,384]{1,0:T(8,128)(2,1)} %get-tuple-element.48), channel_id=1, source_target_pairs={{0,1},{1,2},{2,3},{3,0},{4,5},{5,6},{6,7},{7,4},{8,9},{9,10},{10,1... | collective-permute-start | bytes 1769480 | tf_op jit(solution)/shard_map/ppermute | solution.py:41
  162.0 29.2 %collective-permute-start.19 = (bf16[768,384]{1,0:T(8,128)(2,1)}, bf16[768,384]{1,0:T(8,128)(2,1)S(1)}, u32[]{:S(2)}, u32[]{:S(2)}) collective-permute-start(bf16[768,384]{1,0:T(8,128)(2,1)} %get-tuple-element.49), channel_id=1, source_target_pairs={{0,2},{1,3},{2,0},{3,1},{4,6},{5,7},{6,4},{7,5},{8,10},{9,11},{10,... | collective-permute-start | bytes 1769480 | tf_op jit(solution)/shard_map/ppermute | solution.py:41
  163.4 28.3 %collective-permute-start.20 = (bf16[768,384]{1,0:T(8,128)(2,1)}, bf16[768,384]{1,0:T(8,128)(2,1)S(1)}, u32[]{:S(2)}, u32[]{:S(2)}) collective-permute-start(bf16[768,384]{1,0:T(8,128)(2,1)} %get-tuple-element.50), channel_id=1, source_target_pairs={{0,3},{1,0},{2,1},{3,2},{4,7},{5,4},{6,5},{7,6},{8,11},{9,8},{10,9... | collective-permute-start | bytes 1769480 | tf_op jit(solution)/shard_map/ppermute | solution.py:41
  166.7 11.9 %all-to-all-start.3 = ((bf16[16,16,384]{2,1,0:T(8,128)(2,1)}), bf16[16,16,384]{2,1,0:T(8,128)(2,1)S(1)}, u32[]{:S(2)}, u32[]{:S(2)}) async-start(bf16[16,16,384]{2,1,0:T(8,128)(2,1)} %broadcast_in_dim.5), calls=%async_computation.3 | async-start | bytes 393216 | tf_op jit(solution)/shard_map/all_to_all | solution.py:625
  (12 other events, 65.1 us)
